TPU v7x, 256 devices: a whole 4x4x8 slice. The times are simulated.
256 devices in a mesh: rep: 8 (over z_hi, core), fsdp: 32 (over y, z_lo, x).
Axes of the slice: x: 4, y: 4, z: 8 (z_hi: 4, z_lo: 2; z = z_hi * 2 + z_lo), core: 2. Of those that a mesh axis runs over, the one named last changes fastest.
Arguments:
- tokens: bfloat16 [8, 8192, 4608], P('rep', 'fsdp'), may hold values from -800 to 800
- norm_scale: float32 [8, 4608], P('rep'), may hold values from 0.25 to 1.75
- value_weight: bfloat16 [8, 4608, 1024], P('rep', 'fsdp'), may hold values from -0.09375 to 0.09375
- cotangent: bfloat16 [8, 8192, 1024], P('rep', 'fsdp'), may hold values from -6 to 6
- replica_weights: bfloat16 [8, 2, 4608, 1024], P('rep', None, 'fsdp'), may hold values from -6 to 6
- base: float32 [2, 4608, 1024], P(None, 'fsdp'), may hold values from -6 to 6
- momentum: float32 [2, 4608, 1024], P(None, 'fsdp'), may hold values from -4 to 4
- fragment: int32 [576], P('fsdp'), may hold values from 0 to 1
Outputs:
- values: bfloat16 [8, 8192, 1024], P('rep', 'fsdp')
- input_grad: bfloat16 [8, 8192, 4608], P('rep', 'fsdp')
- weight_grad: float32 [8, 4608, 1024], P('rep', 'fsdp')
- scale_grad: float32 [8, 4608], P('rep', 'fsdp')
- new_base: float32 [4608, 1024], P('fsdp')
- new_momentum: float32 [4608, 1024], P('fsdp')
All inputs are finite; a program needn't handle non-finite values.
Results may differ from a plain program's by a relative error of at most 0.0049.
Values may be sent and summed in bfloat16 or wider, within the bound.
No kernel may reach another device: no remote copies, remote signals or barrier semaphores. Data moves between devices by JAX's collectives and lax.ppermute only.
A program may use at most 128 MiB of HBM per device.

v0:
```python
import functools
import math

import jax
import jax.numpy as jnp
from jax import lax
from jax.experimental import pallas as pl
from jax.experimental.pallas import tpu as pltpu
from jax.sharding import PartitionSpec as P

D = 4608
HV = 1024
ROWS = 144
HALF = D // 2
TOK = 256
NX, NY, NZ = 4, 4, 2
F32, BF16 = jnp.float32, jnp.bfloat16


def fsdp_perm(move):
    pairs = []
    for y in range(NY):
        for z in range(NZ):
            for x in range(NX):
                a, b, c = move(y, z, x)
                pairs.append(((y * NZ + z) * NX + x, (a % NY * NZ + b % NZ) * NX + c % NX))
    return pairs


def after(v, *others):
    return lax.optimization_barrier((v, *others))[0]


def send_x(v, d):
    return lax.ppermute(v, "fsdp", fsdp_perm(lambda y, z, x: (y, z, x + d)))


def send_y(v, d):
    return lax.ppermute(v, "fsdp", fsdp_perm(lambda y, z, x: (y + d, z, x)))


def send_z(v):
    return lax.ppermute(v, "fsdp", fsdp_perm(lambda y, z, x: (y, z + 1, x)))


def send_core(v):
    return lax.ppermute(v, "rep", [(i, i ^ 1) for i in range(8)])


def send_zhi_swap(v, d):
    return lax.ppermute(v, "rep", [(2 * h + c, (h ^ d) * 2 + c) for h in range(4) for c in range(2)])


def kernel_call(kernel, name, out_shape, limit, places, out_places, flops=0, scratch=(), aliases=None):
    spaces = {"v": pltpu.VMEM, "s": pltpu.SMEM, "a": pl.ANY, "h": pltpu.HBM}

    def call(*args):
        count = sum(math.prod(a.shape) * a.dtype.itemsize for a in (*args, *out_shape))
        return pl.pallas_call(
            kernel,
            out_shape=out_shape,
            in_specs=[pl.BlockSpec(memory_space=spaces[p]) for p in places],
            out_specs=[pl.BlockSpec(memory_space=spaces[p]) for p in out_places],
            scratch_shapes=list(scratch),
            input_output_aliases=aliases or {},
            compiler_params=pltpu.CompilerParams(vmem_limit_bytes=limit << 20),
            cost_estimate=pl.CostEstimate(flops=flops, bytes_accessed=2 * count, transcendentals=0),
            name=name,
        )(*args)

    return call


def struct(shape, dtype=BF16):
    return jax.ShapeDtypeStruct(shape, dtype)


RUN = D // (NY * NZ)
CHUNKS = HALF // 256


def pack(out, runs, wide=None):
    line = jnp.concatenate(runs, axis=1)
    for c in range(CHUNKS):
        out[c] = line[:, c * 256 : c * 256 + 256].astype(BF16)
    if wide is not None:
        for j in range(4):
            out[9 + j] = wide[:, j * 256 : j * 256 + 256].astype(BF16)


def unpack_run(ref, r):
    parts = []
    for c in range(r * RUN // 256, (r * RUN + RUN - 1) // 256 + 1):
        first, last = max(r * RUN - c * 256, 0), min(r * RUN + RUN - c * 256, 256)
        parts.append(ref[c][:, first:last])
    return jnp.concatenate(parts, axis=1)


def packed_rows(x, r, dx):
    return pl.ds(pl.multiple_of(r * RUN + lax.rem(x + dx, NX) * ROWS, 16), ROWS)


def sides_of(z, both):
    low, high = both[:, :RUN], both[:, RUN:]
    return jnp.where(z == 0, low, high), jnp.where(z == 0, high, low)


def run_span(y, r):
    return pl.ds(pl.multiple_of(lax.rem(y + r, NY) * (2 * RUN), 128), 2 * RUN)


def inverse_of(tok_ref):
    total = jnp.zeros((TOK, 128), F32)
    for k in range(D // 128):
        part = tok_ref[:, k * 128 : (k + 1) * 128].astype(F32)
        total = total + part * part
    return lax.rsqrt(jnp.sum(total, axis=1, keepdims=True) * (1.0 / D) + 1e-06)


def norm_kernel(where_ref, tok_any, scale_any, cot_any, keep_ref, give_ref, tok, scale, cot, sems):
    y, z = where_ref[0], where_ref[1]
    copies = [
        pltpu.make_async_copy(tok_any.at[:, pl.ds(k * 1152, 1152)], tok.at[:, pl.ds(k * 1152, 1152)], sems.at[k])
        for k in range(4)
    ]
    copies += [
        pltpu.make_async_copy(scale_any, scale, sems.at[4]),
        pltpu.make_async_copy(cot_any, cot, sems.at[5]),
    ]
    for copy in copies:
        copy.start()
    total = jnp.zeros((TOK, 128), F32)
    for k in range(D // 128):
        if k % 9 == 0:
            copies[k // 9].wait()
        part = tok[:, k * 128 : (k + 1) * 128].astype(F32)
        total = total + part * part
    inverse = lax.rsqrt(jnp.sum(total, axis=1, keepdims=True) * (1.0 / D) + 1e-06)
    for copy in copies[4:]:
        copy.wait()
    keep, give = [], []
    for r in range(NY):
        at = run_span(y, r)
        both = (tok[:, at].astype(F32) * inverse * scale[:, at]).astype(BF16)
        mine, other = sides_of(z, both)
        keep.append(mine)
        give.append(other)
    pack(give_ref, give, cot[...])
    pack(keep_ref, keep)


PART, PACK = struct((CHUNKS, TOK, 256)), struct((CHUNKS + 4, TOK, 256))
norm_runs = kernel_call(
    norm_kernel,
    "norm",
    [PART, PACK],
    56,
    "saaa",
    "vv",
    scratch=[
        pltpu.VMEM((TOK, D), BF16),
        pltpu.VMEM((1, D), F32),
        pltpu.VMEM((TOK, HV), BF16),
        pltpu.SemaphoreType.DMA((6,)),
    ],
)


FOUR = struct((4, ROWS, 512))


def grad_kernel(where_ref, *refs):
    arrays, outs, (keep, got, cot, held, in_sems, sems) = refs[:3], refs[3:11], refs[11:]
    x = where_ref[2]
    run_all(
        [
            pltpu.make_async_copy(a, b, in_sems.at[i])
            for i, (a, b) in enumerate(zip(arrays, (keep, got, cot)))
        ]
    )

    def chunk(c):
        mine_t = keep[c].astype(F32).T.astype(BF16)
        other_t = got[c].astype(F32).T.astype(BF16)
        for j in range(4):
            cols = slice(j * 256, j * 256 + 256)
            part = jnp.dot(mine_t, cot[:, cols], preferred_element_type=F32)
            part = part + jnp.dot(other_t, got[9 + j], preferred_element_type=F32)
            held[c * 256 : c * 256 + 256, cols] = part.astype(BF16)

    copies = []
    for c in range(CHUNKS):
        chunk(c)
        if c % 2 or c == 0:
            continue
        r = c // 2 - 1
        for dx in range(NX):
            for half in range(2):
                out = outs[r].at[dx] if half == 0 else outs[4 + dx].at[r]
                copy = pltpu.make_async_copy(
                    held.at[packed_rows(x, r, dx), pl.ds(half * 512, 512)], out, sems.at[len(copies)]
                )
                copy.start()
                copies.append(copy)
    for copy in copies:
        copy.wait()


def run_all(copies):
    for copy in copies:
        copy.start()
    for copy in copies:
        copy.wait()


grad_terms = kernel_call(
    grad_kernel,
    "weight_terms",
    [FOUR] * 8,
    14,
    "saaa",
    "a" * 8,
    flops=2 * HALF * 2 * TOK * HV,
    scratch=[
        pltpu.VMEM(PART.shape, BF16),
        pltpu.VMEM(PACK.shape, BF16),
        pltpu.VMEM((TOK, HV), BF16),
        pltpu.VMEM((HALF, HV), BF16),
        pltpu.SemaphoreType.DMA((3,)),
        pltpu.SemaphoreType.DMA((32,)),
    ],
)


def near_kernel(*refs):
    parts, outs, sems = refs[:8], refs[8:10], refs[10]
    run_all(
        [
            pltpu.make_async_copy(parts[i], outs[i // 4].at[i % 4], sems.at[i])
            for i in range(8)
        ]
    )


make_near = kernel_call(
    near_kernel, "near", [FOUR] * 2, 4, "a" * 8, "aa", scratch=[pltpu.SemaphoreType.DMA((8,))]
)


def middle_kernel(*refs):
    outs, (own, others, sems) = refs[8:16], refs[16:]
    copies = []
    for half in range(2):
        terms = refs[half * 4 : half * 4 + 4]
        for i in (1, 3, 2, 0):
            total = terms[0][i].astype(F32)
            for term in terms[1:]:
                total = total + term[i].astype(F32)
            held = own.at[half] if i == 0 else others.at[half, i - 1]
            held[...] = total.astype(held.dtype)
            copy = pltpu.make_async_copy(held, outs[half * 4 + i], sems.at[half * 4 + i])
            copy.start()
            copies.append(copy)
    for copy in copies:
        copy.wait()


BLOCK = struct((ROWS, 512))
add_ring = kernel_call(
    middle_kernel,
    "add_ring",
    [struct((ROWS, 512), F32), BLOCK, BLOCK, BLOCK] * 2,
    8,
    "v" * 8,
    "a" * 8,
    scratch=[
        pltpu.VMEM((2, ROWS, 512), F32),
        pltpu.VMEM((2, 3, ROWS, 512), BF16),
        pltpu.SemaphoreType.DMA((8,)),
    ],
)
FACTOR = 1.0 / math.sqrt(8192)


def final_kernel(weight_ref, *refs):
    grad_ref, dots_ref = refs[8:]
    dots = jnp.zeros((ROWS, 1), F32)
    for half in range(2):
        own, one, two, three = refs[half * 4 : half * 4 + 4]
        total = own[...] + one[...].astype(F32) + two[...].astype(F32) + three[...].astype(F32)
        total = total * FACTOR
        cols = slice(half * 512, half * 512 + 512)
        grad_ref[:, cols] = total
        dots = dots + jnp.sum(total * weight_ref[:, cols].astype(F32), axis=1, keepdims=True)
    dots_ref[...] = dots


finish_grad = kernel_call(
    final_kernel,
    "finish",
    [struct((ROWS, HV), F32), struct((ROWS, 1), F32)],
    8,
    "v" * 9,
    "vv",
)


def side_kernel(where_ref, scale_ref, cot_ref, runs_ref, *refs):
    packed = runs_ref.shape[0] > CHUNKS
    pieces, outs, (whole, line, sems) = refs[:8], refs[8:-3], refs[-3:]
    y, z, x = where_ref[0], where_ref[1], where_ref[2]
    copies = []
    for r in range(NY):
        for dx in range(NX):
            for half, ref in enumerate((pieces[r].at[dx], pieces[4 + dx].at[r])):
                copy = pltpu.make_async_copy(
                    ref,
                    whole.at[packed_rows(x, r, dx), pl.ds(half * 512, 512)],
                    sems.at[len(copies)],
                )
                copy.start()
                copies.append(copy)
    scales = [sides_of(z, scale_ref[:, run_span(y, r)])[0] for r in range(NY)]
    scales = jnp.concatenate(scales, axis=1)
    for c in range(CHUNKS):
        line[:, c * 256 : c * 256 + 256] = runs_ref[c]
    if packed:
        cot = jnp.concatenate([cot_ref[CHUNKS + j] for j in range(4)], axis=1)
    else:
        cot = cot_ref[...]
    for c in range(CHUNKS):
        if c % 2 == 0 and c < 8:
            for copy in copies[4 * c : 4 * c + 8]:
                copy.wait()
        back = lax.dot_general(
            cot,
            whole[c * 256 : c * 256 + 256, :],
            (((1,), (1,)), ((), ())),
            preferred_element_type=F32,
        )
        outs[0][c] = (back * scales[:, c * 256 : c * 256 + 256]).astype(outs[0].dtype)
    for j in range(4):
        cols = slice(j * 256, j * 256 + 256)
        part = jnp.dot(line[...], whole[:, cols], preferred_element_type=F32)
        if packed:
            outs[0][CHUNKS + j] = part.astype(BF16)
        else:
            outs[1][:, cols] = part


def side_step(name, out_shape, places):
    return kernel_call(
        side_kernel,
        name,
        out_shape,
        14,
        "svvv" + "a" * 8,
        places,
        flops=4 * TOK * HALF * HV,
        scratch=[
            pltpu.VMEM((HALF, HV), BF16),
            pltpu.VMEM((TOK, HALF), BF16),
            pltpu.SemaphoreType.DMA((32,)),
        ],
    )


partner_side = side_step("partner_side", [PACK], "v")
own_side = side_step("own_side", [struct(PART.shape, F32), struct((TOK, HV), F32)], "vv")


def join_kernel(
    where_ref, tok_ref, back_any, part_any, got_ref, val_ref, grad_ref, whole, back, part, sems
):
    y, z = where_ref[0], where_ref[1]
    copies = [
        pltpu.make_async_copy(back_any, back, sems.at[0]),
        pltpu.make_async_copy(part_any, part, sems.at[1]),
    ]
    for copy in copies:
        copy.start()
    inverse = inverse_of(tok_ref)
    for copy in copies:
        copy.wait()
    sums = jnp.zeros((TOK, 128), F32)
    for r in range(NY):
        mine, other = unpack_run(back, r), unpack_run(got_ref, r).astype(F32)
        low, high = jnp.where(z == 0, mine, other), jnp.where(z == 0, other, mine)
        at = run_span(y, r)
        both = jnp.concatenate([low, high], axis=1)
        whole[:, at] = both
        mixed = both * tok_ref[:, at].astype(F32)
        for k in range(9):
            sums = sums + mixed[:, k * 128 : k * 128 + 128]
    lean = inverse * inverse * (jnp.sum(sums, axis=1, keepdims=True) * (1.0 / D))
    for k in range(0, D, 512):
        at = slice(k, k + 512)
        grad = inverse * (whole[:, at] - tok_ref[:, at].astype(F32) * lean)
        grad_ref[:, at] = grad.astype(BF16)
    for j in range(4):
        cols = slice(j * 256, j * 256 + 256)
        val_ref[:, cols] = (part[:, cols] + got_ref[CHUNKS + j].astype(F32)).astype(BF16)


join_sides = kernel_call(
    join_kernel,
    "join_sides",
    [struct((TOK, HV)), struct((TOK, D))],
    24,
    "svaav",
    "vv",
    scratch=[
        pltpu.VMEM((TOK, D), F32),
        pltpu.VMEM(PART.shape, F32),
        pltpu.VMEM((TOK, HV), F32),
        pltpu.SemaphoreType.DMA((2,)),
    ],
)


def pick(stack, row_frag):
    return jnp.where(row_frag[:, None] == 1, stack[1], stack[0])


def outer_start(replica_weights, base, fragment):
    row_frag = jnp.repeat(fragment, 8)
    pseudo = (pick(replica_weights[0], row_frag).astype(F32) - pick(base, row_frag)).astype(BF16)
    core = lax.axis_index("rep") % 2
    keep = lax.dynamic_slice_in_dim(pseudo, core * 512, 512, 1)
    got = send_core(lax.dynamic_slice_in_dim(pseudo, (1 - core) * 512, 512, 1))
    return keep.astype(F32) + got.astype(F32)


def outer_end(total, base, momentum, fragment):
    row_frag = jnp.repeat(fragment, 8)
    core = lax.axis_index("rep") % 2
    mine = total / 8
    theirs = send_core(mine)
    delta = jnp.where(
        core == 0,
        jnp.concatenate([mine, theirs], axis=1),
        jnp.concatenate([theirs, mine], axis=1),
    )
    new_momentum = 0.9 * pick(momentum, row_frag) + delta
    new_base = pick(base, row_frag) + 0.7 * (delta + 0.9 * new_momentum)
    return new_base, new_momentum


def add_zhi(total, d):
    return total + send_zhi_swap(total.astype(BF16), d).astype(F32)


def sides(own, send):
    return send(own, -1), send(own, 1)


def around(own, send, near=None):
    right, left = near or sides(own, send)
    return [own, right, send(after(own, right), 2), left]


def collect(blocks, send):
    one, three = send(blocks[1], 1), send(blocks[3], -1)
    return [blocks[0], one, send(after(blocks[2], one), 2), three]


def per_device(
    tokens, norm_scale, value_weight, cotangent, replica_weights, base, momentum, fragment
):
    tokens, weight, cot = tokens[0], value_weight[0], cotangent[0]
    me = lax.axis_index("fsdp")
    where = jnp.stack([me // (NZ * NX), me // NX % NZ, me % NX]).astype(jnp.int32)
    rings = ((send_x, send_y), (send_y, send_x))

    own = [weight[:, half * 512 : half * 512 + 512] for half in range(2)]
    first_steps = [sides(own[half], rings[half][0]) for half in range(2)]
    keep, give = norm_runs(where, tokens, norm_scale, cot)
    got = send_z(give)
    pair_sum = outer_start(replica_weights, base, fragment)

    parts = []
    for half, (first, _) in enumerate(rings):
        parts += around(after(own[half], give, pair_sum), first, first_steps[half])
    near = make_near(*parts)
    pieces = []
    for n, (_, second) in zip(near, rings):
        pieces += around(n, second)

    terms = grad_terms(where, keep, got, cot)
    sums = []
    for half, (_, second) in enumerate(rings):
        sums += collect(terms[half * 4 : half * 4 + 4], second)
    total = add_zhi(add_zhi(after(pair_sum, got), 1), 2)

    late = after(got, terms[0])
    (packed,) = partner_side(where, norm_scale, late, late, *pieces)
    back = send_z(after(packed, total))
    own_back, own_values = own_side(where, norm_scale, after(cot, packed), keep, *pieces)

    sums = add_ring(*sums)
    last = []
    for half, (first, _) in enumerate(rings):
        last += collect(sums[half * 4 : half * 4 + 4], first)
    values, input_grad = join_sides(where, tokens, own_back, own_values, back)
    weight_grad, dots = finish_grad(after(weight, values), *last)
    scale_grad = dots[:, 0] / lax.dynamic_slice_in_dim(norm_scale[0], me * ROWS, ROWS)
    new_base, new_momentum = outer_end(after(total, own_back), base, momentum, fragment)
    return (
        values[None],
        input_grad[None],
        weight_grad[None],
        scale_grad[None],
        new_base,
        new_momentum,
    )


def solution(mesh):
    in_specs = (
        P("rep", "fsdp", None),
        P("rep", None),
        P("rep", "fsdp", None),
        P("rep", "fsdp", None),
        P("rep", None, "fsdp", None),
        P(None, "fsdp", None),
        P(None, "fsdp", None),
        P("fsdp"),
    )
    out_specs = (
        P("rep", "fsdp", None),
        P("rep", "fsdp", None),
        P("rep", "fsdp", None),
        P("rep", "fsdp"),
        P("fsdp", None),
        P("fsdp", None),
    )
    return jax.shard_map(
        per_device, mesh=mesh, in_specs=in_specs, out_specs=out_specs, check_vma=False
    )
```

profile of v0, /device:TPU:64, one launch (start us, length us, event | category | flops | bytes accessed | tf_op | source)
XLA Modules:
  0.0 127.0 jit_solution(8257286978170599253)
XLA Ops:
  1.3 5.2 %norm.1 = (bf16[9,256,256]{2,1,0:T(8,128)(2,1)}, bf16[13,256,256]{2,1,0:T(8,128)(2,1)}) custom-call(s32[3]{0:T(128)} %pad_add_fusion.where_ref, bf16[256,4608]{1,0:T(8,128)(2,1)} %bitcast.38, f32[1,4608]{1,0:T(1,128)} %scale_ref.3, bf16[256,1024]{1,0:T(8,128)(2,1)} %bitcast.42), custom_call_target="tpu_custom_call" | custom-call | bytes 11571224 | tf_op jit(solution)/shard_map/norm/pallas_call | solution.py:59
  6.5 2.0 %collective-permute-start = (bf16[13,256,256]{2,1,0:T(8,128)(2,1)}, bf16[13,256,256]{2,1,0:T(8,128)(2,1)S(1)}, u32[]{:S(2)}, u32[]{:S(2)}) collective-permute-start(bf16[13,256,256]{2,1,0:T(8,128)(2,1)} %get-tuple-element.48), channel_id=1, source_target_pairs={{0,4},{1,5},{2,6},{3,7},{4,0},{5,1},{6,2},{7,3},{8,12},{9,13},{10,... | collective-permute-start | bytes 5111816 | tf_op jit(solution)/shard_map/ppermute | solution.py:43
  10.8 1.7 %collective-permute-start.7 = (bf16[144,512]{1,0:T(8,128)(2,1)S(1)}, bf16[144,512]{1,0:T(8,128)(2,1)S(1)}, u32[]{:S(2)}, u32[]{:S(2)}) collective-permute-start(bf16[144,512]{1,0:T(8,128)(2,1)S(1)} %get-tuple-element.55.refs_4_), channel_id=1, source_target_pairs={{0,8},{1,9},{2,10},{3,11},{4,12},{5,13},{6,14},{7,15},{8,16},{9,17... | collective-permute-start | bytes 442376 | tf_op jit(solution)/shard_map/ppermute | solution.py:39
  12.5 1.7 %collective-permute-start.5 = (bf16[144,512]{1,0:T(8,128)(2,1)S(1)}, bf16[144,512]{1,0:T(8,128)(2,1)S(1)}, u32[]{:S(2)}, u32[]{:S(2)}) collective-permute-start(bf16[144,512]{1,0:T(8,128)(2,1)S(1)} %get-tuple-element.55.refs_4_), channel_id=1, source_target_pairs={{0,24},{1,25},{2,26},{3,27},{4,28},{5,29},{6,30},{7,31},{8,0},{9,1... | collective-permute-start | bytes 442376 | tf_op jit(solution)/shard_map/ppermute | solution.py:39
  14.2 1.5 %collective-permute-start.4 = (bf16[144,512]{1,0:T(8,128)(2,1)S(1)}, bf16[144,512]{1,0:T(8,128)(2,1)S(1)}, u32[]{:S(2)}, u32[]{:S(2)}) collective-permute-start(bf16[144,512]{1,0:T(8,128)(2,1)S(1)} %get-tuple-element.53.refs_0_), channel_id=1, source_target_pairs={{0,1},{1,2},{2,3},{3,0},{4,5},{5,6},{6,7},{7,4},{8,9},{9,10},{10,1... | collective-permute-start | bytes 442376 | tf_op jit(solution)/shard_map/ppermute | solution.py:35
  15.7 1.7 %collective-permute-start.2 = (bf16[144,512]{1,0:T(8,128)(2,1)S(1)}, bf16[144,512]{1,0:T(8,128)(2,1)S(1)}, u32[]{:S(2)}, u32[]{:S(2)}) collective-permute-start(bf16[144,512]{1,0:T(8,128)(2,1)S(1)} %get-tuple-element.53.refs_0_), channel_id=1, source_target_pairs={{0,3},{1,0},{2,1},{3,2},{4,7},{5,4},{6,5},{7,6},{8,11},{9,8},{10,9... | collective-permute-start | bytes 442376 | tf_op jit(solution)/shard_map/ppermute | solution.py:35
  18.5 2.7 %collective-permute-done.2.refs_1_ = bf16[144,512]{1,0:T(8,128)(2,1)S(1)} collective-permute-done((bf16[144,512]{1,0:T(8,128)(2,1)S(1)}, bf16[144,512]{1,0:T(8,128)(2,1)S(1)}, u32[]{:S(2)}, u32[]{:S(2)}) %collective-permute-start.2) | collective-permute-done | bytes 147488 | tf_op jit(solution)/shard_map/ppermute | solution.py:35
  21.2 2.7 %collective-permute-start.3 = (bf16[144,512]{1,0:T(8,128)(2,1)S(1)}, bf16[144,512]{1,0:T(8,128)(2,1)S(1)}, u32[]{:S(2)}, u32[]{:S(2)}) collective-permute-start(bf16[144,512]{1,0:T(8,128)(2,1)S(1)} %get-tuple-element.53.refs_0_), channel_id=1, source_target_pairs={{0,2},{1,3},{2,0},{3,1},{4,6},{5,7},{6,4},{7,5},{8,10},{9,11},{10,... | collective-permute-start | bytes 442376 | tf_op jit(solution)/shard_map/ppermute | solution.py:35
  24.0 1.8 %collective-permute-start.6 = (bf16[144,512]{1,0:T(8,128)(2,1)S(1)}, bf16[144,512]{1,0:T(8,128)(2,1)S(1)}, u32[]{:S(2)}, u32[]{:S(2)}) collective-permute-start(bf16[144,512]{1,0:T(8,128)(2,1)S(1)} %get-tuple-element.55.refs_4_), channel_id=1, source_target_pairs={{0,16},{1,17},{2,18},{3,19},{4,20},{5,21},{6,22},{7,23},{8,24},{9,... | collective-permute-start | bytes 442376 | tf_op jit(solution)/shard_map/ppermute | solution.py:39
  25.8 2.1 %collective-permute-done.3.refs_2_ = bf16[144,512]{1,0:T(8,128)(2,1)S(1)} collective-permute-done((bf16[144,512]{1,0:T(8,128)(2,1)S(1)}, bf16[144,512]{1,0:T(8,128)(2,1)S(1)}, u32[]{:S(2)}, u32[]{:S(2)}) %collective-permute-start.3) | collective-permute-done | bytes 147488 | tf_op jit(solution)/shard_map/ppermute | solution.py:35
  27.9 2.7 %collective-permute-done.6.refs_6_ = bf16[144,512]{1,0:T(8,128)(2,1)S(1)} collective-permute-done((bf16[144,512]{1,0:T(8,128)(2,1)S(1)}, bf16[144,512]{1,0:T(8,128)(2,1)S(1)}, u32[]{:S(2)}, u32[]{:S(2)}) %collective-permute-start.6) | collective-permute-done | bytes 147488 | tf_op jit(solution)/shard_map/ppermute | solution.py:39
  30.6 1.6 %near.1 = (bf16[4,144,512]{2,1,0:T(8,128)(2,1)S(1)}, bf16[4,144,512]{2,1,0:T(8,128)(2,1)S(1)}) custom-call(bf16[144,512]{1,0:T(8,128)(2,1)S(1)} %get-tuple-element.53.refs_0_, bf16[144,512]{1,0:T(8,128)(2,1)S(1)} %collective-permute-done.2.refs_1_, bf16[144,512]{1,0:T(8,128)(2,1)S(1)} %collective-permute-done.3.refs_2_, ...), custom_call_target="tpu_custom_call" | custom-call | bytes 4718592 | tf_op jit(solution)/shard_map/near/pallas_call | solution.py:59
  32.2 1.7 %collective-permute-start.8 = (bf16[4,144,512]{2,1,0:T(8,128)(2,1)S(1)}, bf16[4,144,512]{2,1,0:T(8,128)(2,1)S(1)}, u32[]{:S(2)}, u32[]{:S(2)}) collective-permute-start(bf16[4,144,512]{2,1,0:T(8,128)(2,1)S(1)} %get-tuple-element.57.refs_0_), channel_id=1, source_target_pairs={{0,24},{1,25},{2,26},{3,27},{4,28},{5,29},{6,30},{7,31},{8,0},{9,1... | collective-permute-start | bytes 1769480 | tf_op jit(solution)/shard_map/ppermute | solution.py:39
  33.9 1.4 %collective-permute-start.11 = (bf16[4,144,512]{2,1,0:T(8,128)(2,1)S(1)}, bf16[4,144,512]{2,1,0:T(8,128)(2,1)S(1)}, u32[]{:S(2)}, u32[]{:S(2)}) collective-permute-start(bf16[4,144,512]{2,1,0:T(8,128)(2,1)S(1)} %get-tuple-element.59.refs_4_), channel_id=1, source_target_pairs={{0,3},{1,0},{2,1},{3,2},{4,7},{5,4},{6,5},{7,6},{8,11},{9,8},{10,9... | collective-permute-start | bytes 1769480 | tf_op jit(solution)/shard_map/ppermute | solution.py:35
  36.3 8.7 %collective-permute-done.8.refs_1_ = bf16[4,144,512]{2,1,0:T(8,128)(2,1)S(1)} collective-permute-done((bf16[4,144,512]{2,1,0:T(8,128)(2,1)S(1)}, bf16[4,144,512]{2,1,0:T(8,128)(2,1)S(1)}, u32[]{:S(2)}, u32[]{:S(2)}) %collective-permute-start.8) | collective-permute-done | bytes 589856 | tf_op jit(solution)/shard_map/ppermute | solution.py:39
  45.0 1.8 %collective-permute-start.9 = (bf16[4,144,512]{2,1,0:T(8,128)(2,1)S(1)}, bf16[4,144,512]{2,1,0:T(8,128)(2,1)S(1)}, u32[]{:S(2)}, u32[]{:S(2)}) collective-permute-start(bf16[4,144,512]{2,1,0:T(8,128)(2,1)S(1)} %get-tuple-element.57.refs_0_), channel_id=1, source_target_pairs={{0,16},{1,17},{2,18},{3,19},{4,20},{5,21},{6,22},{7,23},{8,24},{9,... | collective-permute-start | bytes 1769480 | tf_op jit(solution)/shard_map/ppermute | solution.py:39
  48.0 5.5 %weight_terms.1 = (bf16[4,144,512]{2,1,0:T(8,128)(2,1)S(1)}, bf16[4,144,512]{2,1,0:T(8,128)(2,1)S(1)}, bf16[4,144,512]{2,1,0:T(8,128)(2,1)S(1)}, bf16[4,144,512]...) custom-call(s32[3]{0:T(128)S(1)} %copy-done.6, ...), custom_call_target="tpu_custom_call" | custom-call | flops 2415919104 | bytes 16252952 | tf_op jit(solution)/shard_map/weight_terms/pallas_call | solution.py:59
  54.1 5.4 %collective-permute-start.15 = (bf16[144,512]{1,0:T(8,128)(2,1)S(1)}, bf16[144,512]{1,0:T(8,128)(2,1)S(1)}, u32[]{:S(2)}, u32[]{:S(2)}) collective-permute-start(bf16[144,512]{1,0:T(8,128)(2,1)S(1)} %fusion.2), channel_id=1, source_target_pairs={{0,128},{32,160},{64,192},{96,224},{128,0},{160,32},{192,64},{224,... | collective-permute-start | bytes 442376 | tf_op jit(solution)/shard_map/ppermute | solution.py:51
  59.6 2.0 %collective-permute-done.10.refs_3_ = bf16[4,144,512]{2,1,0:T(8,128)(2,1)S(1)} collective-permute-done((bf16[4,144,512]{2,1,0:T(8,128)(2,1)S(1)}, bf16[4,144,512]{2,1,0:T(8,128)(2,1)S(1)}, u32[]{:S(2)}, u32[]{:S(2)}) %collective-permute-start.10) | collective-permute-done | bytes 589856 | tf_op jit(solution)/shard_map/ppermute | solution.py:39
  61.8 6.3 %partner_side.1 = bf16[13,256,256]{2,1,0:T(8,128)(2,1)} custom-call(s32[3]{0:T(128)S(1)} %copy-done.6, f32[1,4608]{1,0:T(1,128)S(1)} %copy-done.5, bf16[13,256,256]{2,1,0:T(8,128)(2,1)S(1)} %collective-permute-done.refs_1_.cot_ref.runs_ref, bf16[13,256,256]{2,1,0:T(8,128)(2,1)S(1)} %collective-permute-done.refs_1_.cot_ref.runs_ref, ...), custom_call_target="tpu_custom_call" | custom-call | flops 2415919104 | bytes 19697688 | tf_op jit(solution)/shard_map/partner_side/pallas_call | solution.py:59
  69.7 2.0 %collective-permute-start.20 = (bf16[4,144,512]{2,1,0:T(8,128)(2,1)S(1)}, bf16[4,144,512]{2,1,0:T(8,128)(2,1)S(1)}, u32[]{:S(2)}, u32[]{:S(2)}) collective-permute-start(bf16[4,144,512]{2,1,0:T(8,128)(2,1)S(1)} %get-tuple-element.73), channel_id=1, source_target_pairs={{0,1},{1,2},{2,3},{3,0},{4,5},{5,6},{6,7},{7,4},{8,9},{9,10},{10,1... | collective-permute-start | bytes 1769480 | tf_op jit(solution)/shard_map/ppermute | solution.py:35
  71.7 3.2 %collective-permute-start.19 = (bf16[4,144,512]{2,1,0:T(8,128)(2,1)S(1)}, bf16[4,144,512]{2,1,0:T(8,128)(2,1)S(1)}, u32[]{:S(2)}, u32[]{:S(2)}) collective-permute-start(bf16[4,144,512]{2,1,0:T(8,128)(2,1)S(1)} %get-tuple-element.71), channel_id=1, source_target_pairs={{0,24},{1,25},{2,26},{3,27},{4,28},{5,29},{6,30},{7,31},{8,0},{9,1... | collective-permute-start | bytes 1769480 | tf_op jit(solution)/shard_map/ppermute | solution.py:39
  75.8 9.2 %collective-permute-done.17.refs_1_ = bf16[4,144,512]{2,1,0:T(8,128)(2,1)S(1)} collective-permute-done((bf16[4,144,512]{2,1,0:T(8,128)(2,1)S(1)}, bf16[4,144,512]{2,1,0:T(8,128)(2,1)S(1)}, u32[]{:S(2)}, u32[]{:S(2)}) %collective-permute-start.17) | collective-permute-done | bytes 589856 | tf_op jit(solution)/shard_map/ppermute | solution.py:39
  86.2 3.7 %collective-permute-start.21 = (bf16[4,144,512]{2,1,0:T(8,128)(2,1)S(1)}, bf16[4,144,512]{2,1,0:T(8,128)(2,1)S(1)}, u32[]{:S(2)}, u32[]{:S(2)}) collective-permute-start(bf16[4,144,512]{2,1,0:T(8,128)(2,1)S(1)} %get-tuple-element.75), channel_id=1, source_target_pairs={{0,2},{1,3},{2,0},{3,1},{4,6},{5,7},{6,4},{7,5},{8,10},{9,11},{10,... | collective-permute-start | bytes 1769480 | tf_op jit(solution)/shard_map/ppermute | solution.py:35
  89.9 5.1 %own_side.1 = (f32[9,256,256]{2,1,0:T(8,128)S(1)}, f32[256,1024]{1,0:T(8,128)S(1)}) custom-call(s32[3]{0:T(128)S(1)} %copy-done.6, f32[1,4608]{1,0:T(1,128)S(1)} %copy-done.5, bf16[256,1024]{1,0:T(8,128)(2,1)S(1)} %bitcast.44, bf16[9,256,256]{2,1,0:T(8,128)(2,1)S(1)} %copy-done.7, bf16[4,144,512]{2,1,0:T(8,128)(2,1)S(1)} %get-tuple-element.57.refs_0_, ...), custom_call_target="tpu_custom_call" | custom-call | flops 2415919104 | bytes 19697688 | tf_op jit(solution)/shard_map/own_side/pallas_call | solution.py:59
  95.9 4.1 %collective-permute-done.18.refs_2_ = bf16[4,144,512]{2,1,0:T(8,128)(2,1)S(1)} collective-permute-done((bf16[4,144,512]{2,1,0:T(8,128)(2,1)S(1)}, bf16[4,144,512]{2,1,0:T(8,128)(2,1)S(1)}, u32[]{:S(2)}, u32[]{:S(2)}) %collective-permute-start.18) | collective-permute-done | bytes 589856 | tf_op jit(solution)/shard_map/ppermute | solution.py:39
  101.2 1.5 %add_ring.1 = (f32[144,512]{1,0:T(8,128)S(1)}, bf16[144,512]{1,0:T(8,128)(2,1)}, bf16[144,512]{1,0:T(8,128)(2,1)S(1)}, bf16[144,512]{1,0:T(8,128)(2,1)S(1)}, f32...) custom-call(bf16[4,144,512]{2,1,0:T(8,128)(2,1)S(1)} %get-tuple-elem, ...), custom_call_target="tpu_custom_call" | custom-call | bytes 12386304 | tf_op jit(solution)/shard_map/add_ring/pallas_call | solution.py:59
  104.5 2.6 %collective-permute-start.25 = (bf16[144,512]{1,0:T(8,128)(2,1)}, bf16[144,512]{1,0:T(8,128)(2,1)S(1)}, u32[]{:S(2)}, u32[]{:S(2)}) collective-permute-start(bf16[144,512]{1,0:T(8,128)(2,1)} %copy-done.11), channel_id=1, source_target_pairs={{0,3},{1,0},{2,1},{3,2},{4,7},{5,4},{6,5},{7,6},{8,11},{9,8},{10,9... | collective-permute-start | bytes 442376 | tf_op jit(solution)/shard_map/ppermute | solution.py:35
  107.1 2.3 %collective-permute-done.23.refs_1_ = bf16[144,512]{1,0:T(8,128)(2,1)S(1)} collective-permute-done((bf16[144,512]{1,0:T(8,128)(2,1)}, bf16[144,512]{1,0:T(8,128)(2,1)S(1)}, u32[]{:S(2)}, u32[]{:S(2)}) %collective-permute-start.23) | collective-permute-done | bytes 147488 | tf_op jit(solution)/shard_map/ppermute | solution.py:35
  110.9 2.5 %collective-permute-start.24 = (bf16[144,512]{1,0:T(8,128)(2,1)}, bf16[144,512]{1,0:T(8,128)(2,1)S(1)}, u32[]{:S(2)}, u32[]{:S(2)}) collective-permute-start(bf16[144,512]{1,0:T(8,128)(2,1)} %copy-done.9), channel_id=1, source_target_pairs={{0,2},{1,3},{2,0},{3,1},{4,6},{5,7},{6,4},{7,5},{8,10},{9,11},{10,... | collective-permute-start | bytes 442376 | tf_op jit(solution)/shard_map/ppermute | solution.py:35
  114.3 3.6 %multiply_add_fusion = (f32[144,1024]{1,0:T(8,128)}, f32[144,1024]{1,0:T(8,128)}) fusion(f32[144,512]{1,0:T(8,128)} %broadcast_multiply_fusion, f32[144,512]{1,0:T(8,128)} %collective-permute-done.29, pred[]{:T(512)S(6)} %eq.25, f32[2,144,1024]{2,1,0:T(8,128)} %param.13, pred[144]{0:T(512)(128)(4,1)S(1)} %eq.24, f32[2,144,1024]{2,1,0:T(8,128)} %param.14), kind=kLoop, calls=%fused_computation.5 | loop fusion | flops 1622016 | bytes 4128913 | tf_op jit(solution)/shard_map/add | solution.py:445
  117.9 6.6 %join_sides.1 = (bf16[256,1024]{1,0:T(8,128)(2,1)}, bf16[256,4608]{1,0:T(8,128)(2,1)}) custom-call(s32[3]{0:T(128)S(1)} %copy-done.6, bf16[256,4608]{1,0:T(8,128)(2,1)S(1)} %bitcast.39, f32[9,256,256]{2,1,0:T(8,128)S(1)} %get-tuple-element.61.back_any, f32[256,1024]{1,0:T(8,128)S(1)} %copy-done.3, bf16[13,256,256]{2,1,0:T(8,128)(2,1)} %collective-permute-done.16.got_ref), custom_call_target="tpu_custom_call" | custom-call | bytes 20709400 | tf_op jit(solution)/shard_map/join_sides/pallas_call | solution.py:59
  (81 shorter events, 19.2 us)
Async XLA Ops:
  6.5 41.2 %collective-permute-start = (bf16[13,256,256]{2,1,0:T(8,128)(2,1)}, bf16[13,256,256]{2,1,0:T(8,128)(2,1)S(1)}, u32[]{:S(2)}, u32[]{:S(2)}) collective-permute-start(bf16[13,256,256]{2,1,0:T(8,128)(2,1)} %get-tuple-element.48), channel_id=1, source_target_pairs={{0,4},{1,5},{2,6},{3,7},{4,0},{5,1},{6,2},{7,3},{8,12},{9,13},{10,... | collective-permute-start | bytes 5111816 | tf_op jit(solution)/shard_map/ppermute | solution.py:43
  10.1 37.9 %copy-start.4 = (bf16[1,256,1024]{2,1,0:T(8,128)(2,1)S(1)}, bf16[1,256,1024]{2,1,0:T(8,128)(2,1)}, u32[]{:S(2)}) copy-start(bf16[1,256,1024]{2,1,0:T(8,128)(2,1)} %param.11) | copy-start | bytes 1572868
  10.1 37.9 %copy-start.6 = (s32[3]{0:T(128)S(1)}, s32[3]{0:T(128)}, u32[]{:S(2)}) copy-start(s32[3]{0:T(128)} %pad_add_fusion.where_ref) | copy-start | bytes 40
  10.8 4.9 %collective-permute-start.1 = (bf16[144,512]{1,0:T(8,128)(2,1)}, bf16[144,512]{1,0:T(8,128)(2,1)}, u32[]{:S(2)}, u32[]{:S(2)}) collective-permute-start(bf16[144,512]{1,0:T(8,128)(2,1)} %constant_dynamic-slice_fusion), channel_id=1, source_target_pairs={{0,32},{32,0},{64,96},{96,64},{128,160},{160,128},{192,224},{224,1... | collective-permute-start | bytes 442376 | tf_op jit(solution)/shard_map/ppermute | solution.py:47
  10.8 14.9 %collective-permute-start.7 = (bf16[144,512]{1,0:T(8,128)(2,1)S(1)}, bf16[144,512]{1,0:T(8,128)(2,1)S(1)}, u32[]{:S(2)}, u32[]{:S(2)}) collective-permute-start(bf16[144,512]{1,0:T(8,128)(2,1)S(1)} %get-tuple-element.55.refs_4_), channel_id=1, source_target_pairs={{0,8},{1,9},{2,10},{3,11},{4,12},{5,13},{6,14},{7,15},{8,16},{9,17... | collective-permute-start | bytes 442376 | tf_op jit(solution)/shard_map/ppermute | solution.py:39
  12.5 6.0 %collective-permute-start.5 = (bf16[144,512]{1,0:T(8,128)(2,1)S(1)}, bf16[144,512]{1,0:T(8,128)(2,1)S(1)}, u32[]{:S(2)}, u32[]{:S(2)}) collective-permute-start(bf16[144,512]{1,0:T(8,128)(2,1)S(1)} %get-tuple-element.55.refs_4_), channel_id=1, source_target_pairs={{0,24},{1,25},{2,26},{3,27},{4,28},{5,29},{6,30},{7,31},{8,0},{9,1... | collective-permute-start | bytes 442376 | tf_op jit(solution)/shard_map/ppermute | solution.py:39
  14.2 11.6 %collective-permute-start.4 = (bf16[144,512]{1,0:T(8,128)(2,1)S(1)}, bf16[144,512]{1,0:T(8,128)(2,1)S(1)}, u32[]{:S(2)}, u32[]{:S(2)}) collective-permute-start(bf16[144,512]{1,0:T(8,128)(2,1)S(1)} %get-tuple-element.53.refs_0_), channel_id=1, source_target_pairs={{0,1},{1,2},{2,3},{3,0},{4,5},{5,6},{6,7},{7,4},{8,9},{9,10},{10,1... | collective-permute-start | bytes 442376 | tf_op jit(solution)/shard_map/ppermute | solution.py:35
  15.7 5.6 %collective-permute-start.2 = (bf16[144,512]{1,0:T(8,128)(2,1)S(1)}, bf16[144,512]{1,0:T(8,128)(2,1)S(1)}, u32[]{:S(2)}, u32[]{:S(2)}) collective-permute-start(bf16[144,512]{1,0:T(8,128)(2,1)S(1)} %get-tuple-element.53.refs_0_), channel_id=1, source_target_pairs={{0,3},{1,0},{2,1},{3,2},{4,7},{5,4},{6,5},{7,6},{8,11},{9,8},{10,9... | collective-permute-start | bytes 442376 | tf_op jit(solution)/shard_map/ppermute | solution.py:35
  21.2 6.6 %collective-permute-start.3 = (bf16[144,512]{1,0:T(8,128)(2,1)S(1)}, bf16[144,512]{1,0:T(8,128)(2,1)S(1)}, u32[]{:S(2)}, u32[]{:S(2)}) collective-permute-start(bf16[144,512]{1,0:T(8,128)(2,1)S(1)} %get-tuple-element.53.refs_0_), channel_id=1, source_target_pairs={{0,2},{1,3},{2,0},{3,1},{4,6},{5,7},{6,4},{7,5},{8,10},{9,11},{10,... | collective-permute-start | bytes 442376 | tf_op jit(solution)/shard_map/ppermute | solution.py:35
  24.0 6.6 %collective-permute-start.6 = (bf16[144,512]{1,0:T(8,128)(2,1)S(1)}, bf16[144,512]{1,0:T(8,128)(2,1)S(1)}, u32[]{:S(2)}, u32[]{:S(2)}) collective-permute-start(bf16[144,512]{1,0:T(8,128)(2,1)S(1)} %get-tuple-element.55.refs_4_), channel_id=1, source_target_pairs={{0,16},{1,17},{2,18},{3,19},{4,20},{5,21},{6,22},{7,23},{8,24},{9,... | collective-permute-start | bytes 442376 | tf_op jit(solution)/shard_map/ppermute | solution.py:39
  32.2 12.8 %collective-permute-start.8 = (bf16[4,144,512]{2,1,0:T(8,128)(2,1)S(1)}, bf16[4,144,512]{2,1,0:T(8,128)(2,1)S(1)}, u32[]{:S(2)}, u32[]{:S(2)}) collective-permute-start(bf16[4,144,512]{2,1,0:T(8,128)(2,1)S(1)} %get-tuple-element.57.refs_0_), channel_id=1, source_target_pairs={{0,24},{1,25},{2,26},{3,27},{4,28},{5,29},{6,30},{7,31},{8,0},{9,1... | collective-permute-start | bytes 1769480 | tf_op jit(solution)/shard_map/ppermute | solution.py:39
  33.9 12.9 %collective-permute-start.11 = (bf16[4,144,512]{2,1,0:T(8,128)(2,1)S(1)}, bf16[4,144,512]{2,1,0:T(8,128)(2,1)S(1)}, u32[]{:S(2)}, u32[]{:S(2)}) collective-permute-start(bf16[4,144,512]{2,1,0:T(8,128)(2,1)S(1)} %get-tuple-element.59.refs_4_), channel_id=1, source_target_pairs={{0,3},{1,0},{2,1},{3,2},{4,7},{5,4},{6,5},{7,6},{8,11},{9,8},{10,9... | collective-permute-start | bytes 1769480 | tf_op jit(solution)/shard_map/ppermute | solution.py:35
  35.3 26.2 %collective-permute-start.10 = (bf16[4,144,512]{2,1,0:T(8,128)(2,1)S(1)}, bf16[4,144,512]{2,1,0:T(8,128)(2,1)S(1)}, u32[]{:S(2)}, u32[]{:S(2)}) collective-permute-start(bf16[4,144,512]{2,1,0:T(8,128)(2,1)S(1)} %get-tuple-element.57.refs_0_), channel_id=1, source_target_pairs={{0,8},{1,9},{2,10},{3,11},{4,12},{5,13},{6,14},{7,15},{8,16},{9,17... | collective-permute-start | bytes 1769480 | tf_op jit(solution)/shard_map/ppermute | solution.py:39
  35.7 26.0 %collective-permute-start.13 = (bf16[4,144,512]{2,1,0:T(8,128)(2,1)S(1)}, bf16[4,144,512]{2,1,0:T(8,128)(2,1)S(1)}, u32[]{:S(2)}, u32[]{:S(2)}) collective-permute-start(bf16[4,144,512]{2,1,0:T(8,128)(2,1)S(1)} %get-tuple-element.59.refs_4_), channel_id=1, source_target_pairs={{0,1},{1,2},{2,3},{3,0},{4,5},{5,6},{6,7},{7,4},{8,9},{9,10},{10,1... | collective-permute-start | bytes 1769480 | tf_op jit(solution)/shard_map/ppermute | solution.py:35
  45.0 16.8 %collective-permute-start.9 = (bf16[4,144,512]{2,1,0:T(8,128)(2,1)S(1)}, bf16[4,144,512]{2,1,0:T(8,128)(2,1)S(1)}, u32[]{:S(2)}, u32[]{:S(2)}) collective-permute-start(bf16[4,144,512]{2,1,0:T(8,128)(2,1)S(1)} %get-tuple-element.57.refs_0_), channel_id=1, source_target_pairs={{0,16},{1,17},{2,18},{3,19},{4,20},{5,21},{6,22},{7,23},{8,24},{9,... | collective-permute-start | bytes 1769480 | tf_op jit(solution)/shard_map/ppermute | solution.py:39
  46.8 14.9 %collective-permute-start.12 = (bf16[4,144,512]{2,1,0:T(8,128)(2,1)S(1)}, bf16[4,144,512]{2,1,0:T(8,128)(2,1)S(1)}, u32[]{:S(2)}, u32[]{:S(2)}) collective-permute-start(bf16[4,144,512]{2,1,0:T(8,128)(2,1)S(1)} %get-tuple-element.59.refs_4_), channel_id=1, source_target_pairs={{0,2},{1,3},{2,0},{3,1},{4,6},{5,7},{6,4},{7,5},{8,10},{9,11},{10,... | collective-permute-start | bytes 1769480 | tf_op jit(solution)/shard_map/ppermute | solution.py:35
  47.7 6.4 %collective-permute-start.14 = (bf16[144,512]{1,0:T(8,128)(2,1)S(1)}, bf16[144,512]{1,0:T(8,128)(2,1)S(1)}, u32[]{:S(2)}, u32[]{:S(2)}) collective-permute-start(bf16[144,512]{1,0:T(8,128)(2,1)S(1)} %convert_element_type.28), channel_id=1, source_target_pairs={{0,64},{32,96},{64,0},{96,32},{128,192},{160,224},{192,128},{224,1... | collective-permute-start | bytes 442376 | tf_op jit(solution)/shard_map/ppermute | solution.py:51
  54.1 14.0 %collective-permute-start.15 = (bf16[144,512]{1,0:T(8,128)(2,1)S(1)}, bf16[144,512]{1,0:T(8,128)(2,1)S(1)}, u32[]{:S(2)}, u32[]{:S(2)}) collective-permute-start(bf16[144,512]{1,0:T(8,128)(2,1)S(1)} %fusion.2), channel_id=1, source_target_pairs={{0,128},{32,160},{64,192},{96,224},{128,0},{160,32},{192,64},{224,... | collective-permute-start | bytes 442376 | tf_op jit(solution)/shard_map/ppermute | solution.py:51
  68.1 49.7 %collective-permute-start.16 = (bf16[13,256,256]{2,1,0:T(8,128)(2,1)}, bf16[13,256,256]{2,1,0:T(8,128)(2,1)}, u32[]{:S(2)}, u32[]{:S(2)}) collective-permute-start(bf16[13,256,256]{2,1,0:T(8,128)(2,1)} %partner_side.1), channel_id=1, source_target_pairs={{0,4},{1,5},{2,6},{3,7},{4,0},{5,1},{6,2},{7,3},{8,12},{9,13},{10,... | collective-permute-start | bytes 5111816 | tf_op jit(solution)/shard_map/ppermute | solution.py:43
  68.6 16.4 %collective-permute-start.17 = (bf16[4,144,512]{2,1,0:T(8,128)(2,1)S(1)}, bf16[4,144,512]{2,1,0:T(8,128)(2,1)S(1)}, u32[]{:S(2)}, u32[]{:S(2)}) collective-permute-start(bf16[4,144,512]{2,1,0:T(8,128)(2,1)S(1)} %get-tuple-element.68), channel_id=1, source_target_pairs={{0,8},{1,9},{2,10},{3,11},{4,12},{5,13},{6,14},{7,15},{8,16},{9,17... | collective-permute-start | bytes 1769480 | tf_op jit(solution)/shard_map/ppermute | solution.py:39
  69.7 16.5 %collective-permute-start.20 = (bf16[4,144,512]{2,1,0:T(8,128)(2,1)S(1)}, bf16[4,144,512]{2,1,0:T(8,128)(2,1)S(1)}, u32[]{:S(2)}, u32[]{:S(2)}) collective-permute-start(bf16[4,144,512]{2,1,0:T(8,128)(2,1)S(1)} %get-tuple-element.73), channel_id=1, source_target_pairs={{0,1},{1,2},{2,3},{3,0},{4,5},{5,6},{6,7},{7,4},{8,9},{9,10},{10,1... | collective-permute-start | bytes 1769480 | tf_op jit(solution)/shard_map/ppermute | solution.py:35
  71.7 24.1 %collective-permute-start.19 = (bf16[4,144,512]{2,1,0:T(8,128)(2,1)S(1)}, bf16[4,144,512]{2,1,0:T(8,128)(2,1)S(1)}, u32[]{:S(2)}, u32[]{:S(2)}) collective-permute-start(bf16[4,144,512]{2,1,0:T(8,128)(2,1)S(1)} %get-tuple-element.71), channel_id=1, source_target_pairs={{0,24},{1,25},{2,26},{3,27},{4,28},{5,29},{6,30},{7,31},{8,0},{9,1... | collective-permute-start | bytes 1769480 | tf_op jit(solution)/shard_map/ppermute | solution.py:39
  75.0 20.9 %collective-permute-start.22 = (bf16[4,144,512]{2,1,0:T(8,128)(2,1)S(1)}, bf16[4,144,512]{2,1,0:T(8,128)(2,1)S(1)}, u32[]{:S(2)}, u32[]{:S(2)}) collective-permute-start(bf16[4,144,512]{2,1,0:T(8,128)(2,1)S(1)} %get-tuple-element.76), channel_id=1, source_target_pairs={{0,3},{1,0},{2,1},{3,2},{4,7},{5,4},{6,5},{7,6},{8,11},{9,8},{10,9... | collective-permute-start | bytes 1769480 | tf_op jit(solution)/shard_map/ppermute | solution.py:35
  85.0 15.0 %collective-permute-start.18 = (bf16[4,144,512]{2,1,0:T(8,128)(2,1)S(1)}, bf16[4,144,512]{2,1,0:T(8,128)(2,1)S(1)}, u32[]{:S(2)}, u32[]{:S(2)}) collective-permute-start(bf16[4,144,512]{2,1,0:T(8,128)(2,1)S(1)} %get-tuple-element.70), channel_id=1, source_target_pairs={{0,16},{1,17},{2,18},{3,19},{4,20},{5,21},{6,22},{7,23},{8,24},{9,... | collective-permute-start | bytes 1769480 | tf_op jit(solution)/shard_map/ppermute | solution.py:39
  86.2 15.0 %collective-permute-start.21 = (bf16[4,144,512]{2,1,0:T(8,128)(2,1)S(1)}, bf16[4,144,512]{2,1,0:T(8,128)(2,1)S(1)}, u32[]{:S(2)}, u32[]{:S(2)}) collective-permute-start(bf16[4,144,512]{2,1,0:T(8,128)(2,1)S(1)} %get-tuple-element.75), channel_id=1, source_target_pairs={{0,2},{1,3},{2,0},{3,1},{4,6},{5,7},{6,4},{7,5},{8,10},{9,11},{10,... | collective-permute-start | bytes 1769480 | tf_op jit(solution)/shard_map/ppermute | solution.py:35
  95.9 17.5 %collective-permute-start.29 = (f32[144,512]{1,0:T(8,128)}, f32[144,512]{1,0:T(8,128)}, u32[]{:S(2)}, u32[]{:S(2)}) collective-permute-start(f32[144,512]{1,0:T(8,128)} %broadcast_multiply_fusion), channel_id=1, source_target_pairs={{0,32},{32,0},{64,96},{96,64},{128,160},{160,128},{192,224},{224,1... | collective-permute-start | bytes 884744 | tf_op jit(solution)/shard_map/ppermute | solution.py:47
  102.8 6.6 %collective-permute-start.23 = (bf16[144,512]{1,0:T(8,128)(2,1)}, bf16[144,512]{1,0:T(8,128)(2,1)S(1)}, u32[]{:S(2)}, u32[]{:S(2)}) collective-permute-start(bf16[144,512]{1,0:T(8,128)(2,1)} %get-tuple-element.78), channel_id=1, source_target_pairs={{0,1},{1,2},{2,3},{3,0},{4,5},{5,6},{6,7},{7,4},{8,9},{9,10},{10,1... | collective-permute-start | bytes 442376 | tf_op jit(solution)/shard_map/ppermute | solution.py:35
  103.7 7.2 %collective-permute-start.26 = (bf16[144,512]{1,0:T(8,128)(2,1)}, bf16[144,512]{1,0:T(8,128)(2,1)S(1)}, u32[]{:S(2)}, u32[]{:S(2)}) collective-permute-start(bf16[144,512]{1,0:T(8,128)(2,1)} %get-tuple-element.83), channel_id=1, source_target_pairs={{0,8},{1,9},{2,10},{3,11},{4,12},{5,13},{6,14},{7,15},{8,16},{9,17... | collective-permute-start | bytes 442376 | tf_op jit(solution)/shard_map/ppermute | solution.py:39
  104.5 20.0 %collective-permute-start.25 = (bf16[144,512]{1,0:T(8,128)(2,1)}, bf16[144,512]{1,0:T(8,128)(2,1)S(1)}, u32[]{:S(2)}, u32[]{:S(2)}) collective-permute-start(bf16[144,512]{1,0:T(8,128)(2,1)} %copy-done.11), channel_id=1, source_target_pairs={{0,3},{1,0},{2,1},{3,2},{4,7},{5,4},{6,5},{7,6},{8,11},{9,8},{10,9... | collective-permute-start | bytes 442376 | tf_op jit(solution)/shard_map/ppermute | solution.py:35
  109.5 15.0 %collective-permute-start.28 = (bf16[144,512]{1,0:T(8,128)(2,1)}, bf16[144,512]{1,0:T(8,128)(2,1)S(1)}, u32[]{:S(2)}, u32[]{:S(2)}) collective-permute-start(bf16[144,512]{1,0:T(8,128)(2,1)} %copy-done.10), channel_id=1, source_target_pairs={{0,24},{1,25},{2,26},{3,27},{4,28},{5,29},{6,30},{7,31},{8,0},{9,1... | collective-permute-start | bytes 442376 | tf_op jit(solution)/shard_map/ppermute | solution.py:39
  110.9 13.6 %collective-permute-start.24 = (bf16[144,512]{1,0:T(8,128)(2,1)}, bf16[144,512]{1,0:T(8,128)(2,1)S(1)}, u32[]{:S(2)}, u32[]{:S(2)}) collective-permute-start(bf16[144,512]{1,0:T(8,128)(2,1)} %copy-done.9), channel_id=1, source_target_pairs={{0,2},{1,3},{2,0},{3,1},{4,6},{5,7},{6,4},{7,5},{8,10},{9,11},{10,... | collective-permute-start | bytes 442376 | tf_op jit(solution)/shard_map/ppermute | solution.py:35
  113.4 11.1 %collective-permute-start.27 = (bf16[144,512]{1,0:T(8,128)(2,1)}, bf16[144,512]{1,0:T(8,128)(2,1)S(1)}, u32[]{:S(2)}, u32[]{:S(2)}) collective-permute-start(bf16[144,512]{1,0:T(8,128)(2,1)} %copy-done.8), channel_id=1, source_target_pairs={{0,16},{1,17},{2,18},{3,19},{4,20},{5,21},{6,22},{7,23},{8,24},{9,... | collective-permute-start | bytes 442376 | tf_op jit(solution)/shard_map/ppermute | solution.py:39
  (13 other events, 90.5 us)
where the time goes:
time: 127 us
  starting transfers between devices  47.3 us (37%)
  waiting for transfers between devices  35.9 us (28%)
  Pallas kernels  32.8 us (26%)
  other arithmetic  8.93 us (7%)
    pallas_call x8, Pallas kernels, call(): pl.pallas_call(kernel, out_shape=out_shape, in_specs=[pl.BlockSpec(memory...  32.8 us
    ppermute x12, waiting for transfers between devices, send_y(): return lax.ppermute(v, 'fsdp', fsdp_perm(lambda y, z, x: (y + d, z, x)))  26.7 us
    ppermute x12, starting transfers between devices, send_x(): return lax.ppermute(v, 'fsdp', fsdp_perm(lambda y, z, x: (y, z, x + d)))  21.3 us
    ppermute x12, starting transfers between devices, send_y(): return lax.ppermute(v, 'fsdp', fsdp_perm(lambda y, z, x: (y + d, z, x)))  17.9 us
    ppermute x12, waiting for transfers between devices, send_x(): return lax.ppermute(v, 'fsdp', fsdp_perm(lambda y, z, x: (y, z, x + d)))  8.66 us
    ppermute x2, starting transfers between devices, send_zhi_swap(): lax.ppermute(v, 'rep', [(2 * h + c, (h ^ d) * 2 + c) for h in range(4) fo...  5.7 us
    add x1, other arithmetic, outer_end(): new_base = pick(base, row_frag) + 0.7 * (delta + 0.9 * new_momentum)  3.59 us
  transfers between devices with their start and end apart: 30, of which 11 were waited for; matrix products, arithmetic and copies ran while one was open for 6% of the time, Pallas kernels for 21%

commit v1 on v0

--- a/solution.py
+++ b/solution.py
@@ -88,11 +88,14 @@
             out[9 + j] = wide[:, j * 256 : j * 256 + 256].astype(BF16)
 
 
-def unpack_run(ref, r):
+STEP = 64
+
+
+def unpack_run(ref, r, at):
     parts = []
     for c in range(r * RUN // 256, (r * RUN + RUN - 1) // 256 + 1):
         first, last = max(r * RUN - c * 256, 0), min(r * RUN + RUN - c * 256, 256)
-        parts.append(ref[c][:, first:last])
+        parts.append(ref[c, at, :][:, first:last])
     return jnp.concatenate(parts, axis=1)
 
 
@@ -379,27 +382,37 @@
     ]
     for copy in copies:
         copy.start()
-    inverse = inverse_of(tok_ref)
     for copy in copies:
         copy.wait()
-    sums = jnp.zeros((TOK, 128), F32)
-    for r in range(NY):
-        mine, other = unpack_run(back, r), unpack_run(got_ref, r).astype(F32)
-        low, high = jnp.where(z == 0, mine, other), jnp.where(z == 0, other, mine)
-        at = run_span(y, r)
-        both = jnp.concatenate([low, high], axis=1)
-        whole[:, at] = both
-        mixed = both * tok_ref[:, at].astype(F32)
-        for k in range(9):
-            sums = sums + mixed[:, k * 128 : k * 128 + 128]
-    lean = inverse * inverse * (jnp.sum(sums, axis=1, keepdims=True) * (1.0 / D))
-    for k in range(0, D, 512):
-        at = slice(k, k + 512)
-        grad = inverse * (whole[:, at] - tok_ref[:, at].astype(F32) * lean)
-        grad_ref[:, at] = grad.astype(BF16)
-    for j in range(4):
-        cols = slice(j * 256, j * 256 + 256)
-        val_ref[:, cols] = (part[:, cols] + got_ref[CHUNKS + j].astype(F32)).astype(BF16)
+
+    def rows(i, _):
+        at = pl.ds(pl.multiple_of(i * STEP, STEP), STEP)
+        total = jnp.zeros((STEP, 128), F32)
+        for k in range(D // 128):
+            toks = tok_ref[at, k * 128 : (k + 1) * 128].astype(F32)
+            total = total + toks * toks
+        inverse = lax.rsqrt(jnp.sum(total, axis=1, keepdims=True) * (1.0 / D) + 1e-06)
+        sums = jnp.zeros((STEP, 128), F32)
+        for r in range(NY):
+            mine, other = unpack_run(back, r, at), unpack_run(got_ref, r, at).astype(F32)
+            low, high = jnp.where(z == 0, mine, other), jnp.where(z == 0, other, mine)
+            span = run_span(y, r)
+            both = jnp.concatenate([low, high], axis=1)
+            whole[:, span] = both
+            mixed = both * tok_ref[at, span].astype(F32)
+            for k in range(9):
+                sums = sums + mixed[:, k * 128 : k * 128 + 128]
+        lean = inverse * inverse * (jnp.sum(sums, axis=1, keepdims=True) * (1.0 / D))
+        for k in range(0, D, 512):
+            cols = slice(k, k + 512)
+            grad = inverse * (whole[:, cols] - tok_ref[at, cols].astype(F32) * lean)
+            grad_ref[at, cols] = grad.astype(BF16)
+        for j in range(4):
+            cols = slice(j * 256, j * 256 + 256)
+            val_ref[at, cols] = (part[at, cols] + got_ref[CHUNKS + j, at, :].astype(F32)).astype(BF16)
+        return 0
+
+    lax.fori_loop(0, TOK // STEP, rows, 0)
 
 
 join_sides = kernel_call(
@@ -410,7 +423,7 @@
     "svaav",
     "vv",
     scratch=[
-        pltpu.VMEM((TOK, D), F32),
+        pltpu.VMEM((STEP, D), F32),
         pltpu.VMEM(PART.shape, F32),
         pltpu.VMEM((TOK, HV), F32),
         pltpu.SemaphoreType.DMA((2,)),

time: 127 us -> 127 us (level)
  no operation moved by 1% of the time
where the time goes in v1:
time: 127 us
  starting transfers between devices  47.3 us (37%)
  waiting for transfers between devices  35.9 us (28%)
  Pallas kernels  33 us (26%)
  other arithmetic  8.93 us (7%)
    pallas_call x8, Pallas kernels, call(): pl.pallas_call(kernel, out_shape=out_shape, in_specs=[pl.BlockSpec(memory...  33 us
    ppermute x12, waiting for transfers between devices, send_y(): return lax.ppermute(v, 'fsdp', fsdp_perm(lambda y, z, x: (y + d, z, x)))  26.7 us
    ppermute x12, starting transfers between devices, send_x(): return lax.ppermute(v, 'fsdp', fsdp_perm(lambda y, z, x: (y, z, x + d)))  21.3 us
    ppermute x12, starting transfers between devices, send_y(): return lax.ppermute(v, 'fsdp', fsdp_perm(lambda y, z, x: (y + d, z, x)))  17.9 us
    ppermute x12, waiting for transfers between devices, send_x(): return lax.ppermute(v, 'fsdp', fsdp_perm(lambda y, z, x: (y, z, x + d)))  8.66 us
    ppermute x2, starting transfers between devices, send_zhi_swap(): lax.ppermute(v, 'rep', [(2 * h + c, (h ^ d) * 2 + c) for h in range(4) fo...  5.7 us
    add x1, other arithmetic, outer_end(): new_base = pick(base, row_frag) + 0.7 * (delta + 0.9 * new_momentum)  3.59 us
  transfers between devices with their start and end apart: 30, of which 11 were waited for; matrix products, arithmetic and copies ran while one was open for 6% of the time, Pallas kernels for 21%

profile of v1, /device:TPU:64, one launch (start us, length us, event | category | flops | bytes accessed | tf_op | source)
XLA Modules:
  0.0 127.2 jit_solution(3445391082811278315)
XLA Ops:
  1.3 5.2 %norm.1 = (bf16[9,256,256]{2,1,0:T(8,128)(2,1)}, bf16[13,256,256]{2,1,0:T(8,128)(2,1)}) custom-call(s32[3]{0:T(128)} %pad_add_fusion.where_ref, bf16[256,4608]{1,0:T(8,128)(2,1)} %bitcast.38, f32[1,4608]{1,0:T(1,128)} %scale_ref.3, bf16[256,1024]{1,0:T(8,128)(2,1)} %bitcast.42), custom_call_target="tpu_custom_call" | custom-call | bytes 11571224 | tf_op jit(solution)/shard_map/norm/pallas_call | solution.py:59
  6.5 2.0 %collective-permute-start = (bf16[13,256,256]{2,1,0:T(8,128)(2,1)}, bf16[13,256,256]{2,1,0:T(8,128)(2,1)S(1)}, u32[]{:S(2)}, u32[]{:S(2)}) collective-permute-start(bf16[13,256,256]{2,1,0:T(8,128)(2,1)} %get-tuple-element.48), channel_id=1, source_target_pairs={{0,4},{1,5},{2,6},{3,7},{4,0},{5,1},{6,2},{7,3},{8,12},{9,13},{10,... | collective-permute-start | bytes 5111816 | tf_op jit(solution)/shard_map/ppermute | solution.py:43
  10.8 1.7 %collective-permute-start.7 = (bf16[144,512]{1,0:T(8,128)(2,1)S(1)}, bf16[144,512]{1,0:T(8,128)(2,1)S(1)}, u32[]{:S(2)}, u32[]{:S(2)}) collective-permute-start(bf16[144,512]{1,0:T(8,128)(2,1)S(1)} %get-tuple-element.55.refs_4_), channel_id=1, source_target_pairs={{0,8},{1,9},{2,10},{3,11},{4,12},{5,13},{6,14},{7,15},{8,16},{9,17... | collective-permute-start | bytes 442376 | tf_op jit(solution)/shard_map/ppermute | solution.py:39
  12.5 1.7 %collective-permute-start.5 = (bf16[144,512]{1,0:T(8,128)(2,1)S(1)}, bf16[144,512]{1,0:T(8,128)(2,1)S(1)}, u32[]{:S(2)}, u32[]{:S(2)}) collective-permute-start(bf16[144,512]{1,0:T(8,128)(2,1)S(1)} %get-tuple-element.55.refs_4_), channel_id=1, source_target_pairs={{0,24},{1,25},{2,26},{3,27},{4,28},{5,29},{6,30},{7,31},{8,0},{9,1... | collective-permute-start | bytes 442376 | tf_op jit(solution)/shard_map/ppermute | solution.py:39
  14.2 1.5 %collective-permute-start.4 = (bf16[144,512]{1,0:T(8,128)(2,1)S(1)}, bf16[144,512]{1,0:T(8,128)(2,1)S(1)}, u32[]{:S(2)}, u32[]{:S(2)}) collective-permute-start(bf16[144,512]{1,0:T(8,128)(2,1)S(1)} %get-tuple-element.53.refs_0_), channel_id=1, source_target_pairs={{0,1},{1,2},{2,3},{3,0},{4,5},{5,6},{6,7},{7,4},{8,9},{9,10},{10,1... | collective-permute-start | bytes 442376 | tf_op jit(solution)/shard_map/ppermute | solution.py:35
  15.7 1.7 %collective-permute-start.2 = (bf16[144,512]{1,0:T(8,128)(2,1)S(1)}, bf16[144,512]{1,0:T(8,128)(2,1)S(1)}, u32[]{:S(2)}, u32[]{:S(2)}) collective-permute-start(bf16[144,512]{1,0:T(8,128)(2,1)S(1)} %get-tuple-element.53.refs_0_), channel_id=1, source_target_pairs={{0,3},{1,0},{2,1},{3,2},{4,7},{5,4},{6,5},{7,6},{8,11},{9,8},{10,9... | collective-permute-start | bytes 442376 | tf_op jit(solution)/shard_map/ppermute | solution.py:35
  18.5 2.7 %collective-permute-done.2.refs_1_ = bf16[144,512]{1,0:T(8,128)(2,1)S(1)} collective-permute-done((bf16[144,512]{1,0:T(8,128)(2,1)S(1)}, bf16[144,512]{1,0:T(8,128)(2,1)S(1)}, u32[]{:S(2)}, u32[]{:S(2)}) %collective-permute-start.2) | collective-permute-done | bytes 147488 | tf_op jit(solution)/shard_map/ppermute | solution.py:35
  21.2 2.7 %collective-permute-start.3 = (bf16[144,512]{1,0:T(8,128)(2,1)S(1)}, bf16[144,512]{1,0:T(8,128)(2,1)S(1)}, u32[]{:S(2)}, u32[]{:S(2)}) collective-permute-start(bf16[144,512]{1,0:T(8,128)(2,1)S(1)} %get-tuple-element.53.refs_0_), channel_id=1, source_target_pairs={{0,2},{1,3},{2,0},{3,1},{4,6},{5,7},{6,4},{7,5},{8,10},{9,11},{10,... | collective-permute-start | bytes 442376 | tf_op jit(solution)/shard_map/ppermute | solution.py:35
  24.0 1.8 %collective-permute-start.6 = (bf16[144,512]{1,0:T(8,128)(2,1)S(1)}, bf16[144,512]{1,0:T(8,128)(2,1)S(1)}, u32[]{:S(2)}, u32[]{:S(2)}) collective-permute-start(bf16[144,512]{1,0:T(8,128)(2,1)S(1)} %get-tuple-element.55.refs_4_), channel_id=1, source_target_pairs={{0,16},{1,17},{2,18},{3,19},{4,20},{5,21},{6,22},{7,23},{8,24},{9,... | collective-permute-start | bytes 442376 | tf_op jit(solution)/shard_map/ppermute | solution.py:39
  25.8 2.1 %collective-permute-done.3.refs_2_ = bf16[144,512]{1,0:T(8,128)(2,1)S(1)} collective-permute-done((bf16[144,512]{1,0:T(8,128)(2,1)S(1)}, bf16[144,512]{1,0:T(8,128)(2,1)S(1)}, u32[]{:S(2)}, u32[]{:S(2)}) %collective-permute-start.3) | collective-permute-done | bytes 147488 | tf_op jit(solution)/shard_map/ppermute | solution.py:35
  27.9 2.7 %collective-permute-done.6.refs_6_ = bf16[144,512]{1,0:T(8,128)(2,1)S(1)} collective-permute-done((bf16[144,512]{1,0:T(8,128)(2,1)S(1)}, bf16[144,512]{1,0:T(8,128)(2,1)S(1)}, u32[]{:S(2)}, u32[]{:S(2)}) %collective-permute-start.6) | collective-permute-done | bytes 147488 | tf_op jit(solution)/shard_map/ppermute | solution.py:39
  30.6 1.6 %near.1 = (bf16[4,144,512]{2,1,0:T(8,128)(2,1)S(1)}, bf16[4,144,512]{2,1,0:T(8,128)(2,1)S(1)}) custom-call(bf16[144,512]{1,0:T(8,128)(2,1)S(1)} %get-tuple-element.53.refs_0_, bf16[144,512]{1,0:T(8,128)(2,1)S(1)} %collective-permute-done.2.refs_1_, bf16[144,512]{1,0:T(8,128)(2,1)S(1)} %collective-permute-done.3.refs_2_, ...), custom_call_target="tpu_custom_call" | custom-call | bytes 4718592 | tf_op jit(solution)/shard_map/near/pallas_call | solution.py:59
  32.2 1.7 %collective-permute-start.8 = (bf16[4,144,512]{2,1,0:T(8,128)(2,1)S(1)}, bf16[4,144,512]{2,1,0:T(8,128)(2,1)S(1)}, u32[]{:S(2)}, u32[]{:S(2)}) collective-permute-start(bf16[4,144,512]{2,1,0:T(8,128)(2,1)S(1)} %get-tuple-element.57.refs_0_), channel_id=1, source_target_pairs={{0,24},{1,25},{2,26},{3,27},{4,28},{5,29},{6,30},{7,31},{8,0},{9,1... | collective-permute-start | bytes 1769480 | tf_op jit(solution)/shard_map/ppermute | solution.py:39
  33.9 1.4 %collective-permute-start.11 = (bf16[4,144,512]{2,1,0:T(8,128)(2,1)S(1)}, bf16[4,144,512]{2,1,0:T(8,128)(2,1)S(1)}, u32[]{:S(2)}, u32[]{:S(2)}) collective-permute-start(bf16[4,144,512]{2,1,0:T(8,128)(2,1)S(1)} %get-tuple-element.59.refs_4_), channel_id=1, source_target_pairs={{0,3},{1,0},{2,1},{3,2},{4,7},{5,4},{6,5},{7,6},{8,11},{9,8},{10,9... | collective-permute-start | bytes 1769480 | tf_op jit(solution)/shard_map/ppermute | solution.py:35
  36.3 8.7 %collective-permute-done.8.refs_1_ = bf16[4,144,512]{2,1,0:T(8,128)(2,1)S(1)} collective-permute-done((bf16[4,144,512]{2,1,0:T(8,128)(2,1)S(1)}, bf16[4,144,512]{2,1,0:T(8,128)(2,1)S(1)}, u32[]{:S(2)}, u32[]{:S(2)}) %collective-permute-start.8) | collective-permute-done | bytes 589856 | tf_op jit(solution)/shard_map/ppermute | solution.py:39
  45.0 1.8 %collective-permute-start.9 = (bf16[4,144,512]{2,1,0:T(8,128)(2,1)S(1)}, bf16[4,144,512]{2,1,0:T(8,128)(2,1)S(1)}, u32[]{:S(2)}, u32[]{:S(2)}) collective-permute-start(bf16[4,144,512]{2,1,0:T(8,128)(2,1)S(1)} %get-tuple-element.57.refs_0_), channel_id=1, source_target_pairs={{0,16},{1,17},{2,18},{3,19},{4,20},{5,21},{6,22},{7,23},{8,24},{9,... | collective-permute-start | bytes 1769480 | tf_op jit(solution)/shard_map/ppermute | solution.py:39
  48.0 5.5 %weight_terms.1 = (bf16[4,144,512]{2,1,0:T(8,128)(2,1)S(1)}, bf16[4,144,512]{2,1,0:T(8,128)(2,1)S(1)}, bf16[4,144,512]{2,1,0:T(8,128)(2,1)S(1)}, bf16[4,144,512]...) custom-call(s32[3]{0:T(128)S(1)} %copy-done.6, ...), custom_call_target="tpu_custom_call" | custom-call | flops 2415919104 | bytes 16252952 | tf_op jit(solution)/shard_map/weight_terms/pallas_call | solution.py:59
  54.1 5.4 %collective-permute-start.15 = (bf16[144,512]{1,0:T(8,128)(2,1)S(1)}, bf16[144,512]{1,0:T(8,128)(2,1)S(1)}, u32[]{:S(2)}, u32[]{:S(2)}) collective-permute-start(bf16[144,512]{1,0:T(8,128)(2,1)S(1)} %fusion.2), channel_id=1, source_target_pairs={{0,128},{32,160},{64,192},{96,224},{128,0},{160,32},{192,64},{224,... | collective-permute-start | bytes 442376 | tf_op jit(solution)/shard_map/ppermute | solution.py:51
  59.6 2.0 %collective-permute-done.10.refs_3_ = bf16[4,144,512]{2,1,0:T(8,128)(2,1)S(1)} collective-permute-done((bf16[4,144,512]{2,1,0:T(8,128)(2,1)S(1)}, bf16[4,144,512]{2,1,0:T(8,128)(2,1)S(1)}, u32[]{:S(2)}, u32[]{:S(2)}) %collective-permute-start.10) | collective-permute-done | bytes 589856 | tf_op jit(solution)/shard_map/ppermute | solution.py:39
  61.8 6.3 %partner_side.1 = bf16[13,256,256]{2,1,0:T(8,128)(2,1)} custom-call(s32[3]{0:T(128)S(1)} %copy-done.6, f32[1,4608]{1,0:T(1,128)S(1)} %copy-done.5, bf16[13,256,256]{2,1,0:T(8,128)(2,1)S(1)} %collective-permute-done.refs_1_.cot_ref.runs_ref, bf16[13,256,256]{2,1,0:T(8,128)(2,1)S(1)} %collective-permute-done.refs_1_.cot_ref.runs_ref, ...), custom_call_target="tpu_custom_call" | custom-call | flops 2415919104 | bytes 19697688 | tf_op jit(solution)/shard_map/partner_side/pallas_call | solution.py:59
  69.7 2.0 %collective-permute-start.20 = (bf16[4,144,512]{2,1,0:T(8,128)(2,1)S(1)}, bf16[4,144,512]{2,1,0:T(8,128)(2,1)S(1)}, u32[]{:S(2)}, u32[]{:S(2)}) collective-permute-start(bf16[4,144,512]{2,1,0:T(8,128)(2,1)S(1)} %get-tuple-element.73), channel_id=1, source_target_pairs={{0,1},{1,2},{2,3},{3,0},{4,5},{5,6},{6,7},{7,4},{8,9},{9,10},{10,1... | collective-permute-start | bytes 1769480 | tf_op jit(solution)/shard_map/ppermute | solution.py:35
  71.7 3.2 %collective-permute-start.19 = (bf16[4,144,512]{2,1,0:T(8,128)(2,1)S(1)}, bf16[4,144,512]{2,1,0:T(8,128)(2,1)S(1)}, u32[]{:S(2)}, u32[]{:S(2)}) collective-permute-start(bf16[4,144,512]{2,1,0:T(8,128)(2,1)S(1)} %get-tuple-element.71), channel_id=1, source_target_pairs={{0,24},{1,25},{2,26},{3,27},{4,28},{5,29},{6,30},{7,31},{8,0},{9,1... | collective-permute-start | bytes 1769480 | tf_op jit(solution)/shard_map/ppermute | solution.py:39
  75.8 9.2 %collective-permute-done.17.refs_1_ = bf16[4,144,512]{2,1,0:T(8,128)(2,1)S(1)} collective-permute-done((bf16[4,144,512]{2,1,0:T(8,128)(2,1)S(1)}, bf16[4,144,512]{2,1,0:T(8,128)(2,1)S(1)}, u32[]{:S(2)}, u32[]{:S(2)}) %collective-permute-start.17) | collective-permute-done | bytes 589856 | tf_op jit(solution)/shard_map/ppermute | solution.py:39
  86.2 3.7 %collective-permute-start.21 = (bf16[4,144,512]{2,1,0:T(8,128)(2,1)S(1)}, bf16[4,144,512]{2,1,0:T(8,128)(2,1)S(1)}, u32[]{:S(2)}, u32[]{:S(2)}) collective-permute-start(bf16[4,144,512]{2,1,0:T(8,128)(2,1)S(1)} %get-tuple-element.75), channel_id=1, source_target_pairs={{0,2},{1,3},{2,0},{3,1},{4,6},{5,7},{6,4},{7,5},{8,10},{9,11},{10,... | collective-permute-start | bytes 1769480 | tf_op jit(solution)/shard_map/ppermute | solution.py:35
  89.9 5.1 %own_side.1 = (f32[9,256,256]{2,1,0:T(8,128)S(1)}, f32[256,1024]{1,0:T(8,128)S(1)}) custom-call(s32[3]{0:T(128)S(1)} %copy-done.6, f32[1,4608]{1,0:T(1,128)S(1)} %copy-done.5, bf16[256,1024]{1,0:T(8,128)(2,1)S(1)} %bitcast.44, bf16[9,256,256]{2,1,0:T(8,128)(2,1)S(1)} %copy-done.7, bf16[4,144,512]{2,1,0:T(8,128)(2,1)S(1)} %get-tuple-element.57.refs_0_, ...), custom_call_target="tpu_custom_call" | custom-call | flops 2415919104 | bytes 19697688 | tf_op jit(solution)/shard_map/own_side/pallas_call | solution.py:59
  95.9 4.1 %collective-permute-done.18.refs_2_ = bf16[4,144,512]{2,1,0:T(8,128)(2,1)S(1)} collective-permute-done((bf16[4,144,512]{2,1,0:T(8,128)(2,1)S(1)}, bf16[4,144,512]{2,1,0:T(8,128)(2,1)S(1)}, u32[]{:S(2)}, u32[]{:S(2)}) %collective-permute-start.18) | collective-permute-done | bytes 589856 | tf_op jit(solution)/shard_map/ppermute | solution.py:39
  101.2 1.5 %add_ring.1 = (f32[144,512]{1,0:T(8,128)S(1)}, bf16[144,512]{1,0:T(8,128)(2,1)}, bf16[144,512]{1,0:T(8,128)(2,1)S(1)}, bf16[144,512]{1,0:T(8,128)(2,1)S(1)}, f32...) custom-call(bf16[4,144,512]{2,1,0:T(8,128)(2,1)S(1)} %get-tuple-elem, ...), custom_call_target="tpu_custom_call" | custom-call | bytes 12386304 | tf_op jit(solution)/shard_map/add_ring/pallas_call | solution.py:59
  104.5 2.6 %collective-permute-start.25 = (bf16[144,512]{1,0:T(8,128)(2,1)}, bf16[144,512]{1,0:T(8,128)(2,1)S(1)}, u32[]{:S(2)}, u32[]{:S(2)}) collective-permute-start(bf16[144,512]{1,0:T(8,128)(2,1)} %copy-done.11), channel_id=1, source_target_pairs={{0,3},{1,0},{2,1},{3,2},{4,7},{5,4},{6,5},{7,6},{8,11},{9,8},{10,9... | collective-permute-start | bytes 442376 | tf_op jit(solution)/shard_map/ppermute | solution.py:35
  107.1 2.3 %collective-permute-done.23.refs_1_ = bf16[144,512]{1,0:T(8,128)(2,1)S(1)} collective-permute-done((bf16[144,512]{1,0:T(8,128)(2,1)}, bf16[144,512]{1,0:T(8,128)(2,1)S(1)}, u32[]{:S(2)}, u32[]{:S(2)}) %collective-permute-start.23) | collective-permute-done | bytes 147488 | tf_op jit(solution)/shard_map/ppermute | solution.py:35
  110.9 2.5 %collective-permute-start.24 = (bf16[144,512]{1,0:T(8,128)(2,1)}, bf16[144,512]{1,0:T(8,128)(2,1)S(1)}, u32[]{:S(2)}, u32[]{:S(2)}) collective-permute-start(bf16[144,512]{1,0:T(8,128)(2,1)} %copy-done.9), channel_id=1, source_target_pairs={{0,2},{1,3},{2,0},{3,1},{4,6},{5,7},{6,4},{7,5},{8,10},{9,11},{10,... | collective-permute-start | bytes 442376 | tf_op jit(solution)/shard_map/ppermute | solution.py:35
  114.3 3.6 %multiply_add_fusion = (f32[144,1024]{1,0:T(8,128)}, f32[144,1024]{1,0:T(8,128)}) fusion(f32[144,512]{1,0:T(8,128)} %broadcast_multiply_fusion, f32[144,512]{1,0:T(8,128)} %collective-permute-done.29, pred[]{:T(512)S(6)} %eq.25, f32[2,144,1024]{2,1,0:T(8,128)} %param.13, pred[144]{0:T(512)(128)(4,1)S(1)} %eq.24, f32[2,144,1024]{2,1,0:T(8,128)} %param.14), kind=kLoop, calls=%fused_computation.5 | loop fusion | flops 1622016 | bytes 4128913 | tf_op jit(solution)/shard_map/add | solution.py:458
  117.9 6.8 %join_sides.1 = (bf16[256,1024]{1,0:T(8,128)(2,1)}, bf16[256,4608]{1,0:T(8,128)(2,1)}) custom-call(s32[3]{0:T(128)S(1)} %copy-done.6, bf16[256,4608]{1,0:T(8,128)(2,1)S(1)} %bitcast.39, f32[9,256,256]{2,1,0:T(8,128)S(1)} %get-tuple-element.61.back_any, f32[256,1024]{1,0:T(8,128)S(1)} %copy-done.3, bf16[13,256,256]{2,1,0:T(8,128)(2,1)} %collective-permute-done.16.got_ref), custom_call_target="tpu_custom_call" | custom-call | bytes 20709400 | tf_op jit(solution)/shard_map/join_sides/pallas_call | solution.py:59
  (81 shorter events, 19.2 us)
Async XLA Ops:
  6.5 41.2 %collective-permute-start = (bf16[13,256,256]{2,1,0:T(8,128)(2,1)}, bf16[13,256,256]{2,1,0:T(8,128)(2,1)S(1)}, u32[]{:S(2)}, u32[]{:S(2)}) collective-permute-start(bf16[13,256,256]{2,1,0:T(8,128)(2,1)} %get-tuple-element.48), channel_id=1, source_target_pairs={{0,4},{1,5},{2,6},{3,7},{4,0},{5,1},{6,2},{7,3},{8,12},{9,13},{10,... | collective-permute-start | bytes 5111816 | tf_op jit(solution)/shard_map/ppermute | solution.py:43
  10.1 37.9 %copy-start.4 = (bf16[1,256,1024]{2,1,0:T(8,128)(2,1)S(1)}, bf16[1,256,1024]{2,1,0:T(8,128)(2,1)}, u32[]{:S(2)}) copy-start(bf16[1,256,1024]{2,1,0:T(8,128)(2,1)} %param.11) | copy-start | bytes 1572868
  10.1 37.9 %copy-start.6 = (s32[3]{0:T(128)S(1)}, s32[3]{0:T(128)}, u32[]{:S(2)}) copy-start(s32[3]{0:T(128)} %pad_add_fusion.where_ref) | copy-start | bytes 40
  10.8 4.9 %collective-permute-start.1 = (bf16[144,512]{1,0:T(8,128)(2,1)}, bf16[144,512]{1,0:T(8,128)(2,1)}, u32[]{:S(2)}, u32[]{:S(2)}) collective-permute-start(bf16[144,512]{1,0:T(8,128)(2,1)} %constant_dynamic-slice_fusion), channel_id=1, source_target_pairs={{0,32},{32,0},{64,96},{96,64},{128,160},{160,128},{192,224},{224,1... | collective-permute-start | bytes 442376 | tf_op jit(solution)/shard_map/ppermute | solution.py:47
  10.8 14.9 %collective-permute-start.7 = (bf16[144,512]{1,0:T(8,128)(2,1)S(1)}, bf16[144,512]{1,0:T(8,128)(2,1)S(1)}, u32[]{:S(2)}, u32[]{:S(2)}) collective-permute-start(bf16[144,512]{1,0:T(8,128)(2,1)S(1)} %get-tuple-element.55.refs_4_), channel_id=1, source_target_pairs={{0,8},{1,9},{2,10},{3,11},{4,12},{5,13},{6,14},{7,15},{8,16},{9,17... | collective-permute-start | bytes 442376 | tf_op jit(solution)/shard_map/ppermute | solution.py:39
  12.5 6.0 %collective-permute-start.5 = (bf16[144,512]{1,0:T(8,128)(2,1)S(1)}, bf16[144,512]{1,0:T(8,128)(2,1)S(1)}, u32[]{:S(2)}, u32[]{:S(2)}) collective-permute-start(bf16[144,512]{1,0:T(8,128)(2,1)S(1)} %get-tuple-element.55.refs_4_), channel_id=1, source_target_pairs={{0,24},{1,25},{2,26},{3,27},{4,28},{5,29},{6,30},{7,31},{8,0},{9,1... | collective-permute-start | bytes 442376 | tf_op jit(solution)/shard_map/ppermute | solution.py:39
  14.2 11.6 %collective-permute-start.4 = (bf16[144,512]{1,0:T(8,128)(2,1)S(1)}, bf16[144,512]{1,0:T(8,128)(2,1)S(1)}, u32[]{:S(2)}, u32[]{:S(2)}) collective-permute-start(bf16[144,512]{1,0:T(8,128)(2,1)S(1)} %get-tuple-element.53.refs_0_), channel_id=1, source_target_pairs={{0,1},{1,2},{2,3},{3,0},{4,5},{5,6},{6,7},{7,4},{8,9},{9,10},{10,1... | collective-permute-start | bytes 442376 | tf_op jit(solution)/shard_map/ppermute | solution.py:35
  15.7 5.6 %collective-permute-start.2 = (bf16[144,512]{1,0:T(8,128)(2,1)S(1)}, bf16[144,512]{1,0:T(8,128)(2,1)S(1)}, u32[]{:S(2)}, u32[]{:S(2)}) collective-permute-start(bf16[144,512]{1,0:T(8,128)(2,1)S(1)} %get-tuple-element.53.refs_0_), channel_id=1, source_target_pairs={{0,3},{1,0},{2,1},{3,2},{4,7},{5,4},{6,5},{7,6},{8,11},{9,8},{10,9... | collective-permute-start | bytes 442376 | tf_op jit(solution)/shard_map/ppermute | solution.py:35
  21.2 6.6 %collective-permute-start.3 = (bf16[144,512]{1,0:T(8,128)(2,1)S(1)}, bf16[144,512]{1,0:T(8,128)(2,1)S(1)}, u32[]{:S(2)}, u32[]{:S(2)}) collective-permute-start(bf16[144,512]{1,0:T(8,128)(2,1)S(1)} %get-tuple-element.53.refs_0_), channel_id=1, source_target_pairs={{0,2},{1,3},{2,0},{3,1},{4,6},{5,7},{6,4},{7,5},{8,10},{9,11},{10,... | collective-permute-start | bytes 442376 | tf_op jit(solution)/shard_map/ppermute | solution.py:35
  24.0 6.6 %collective-permute-start.6 = (bf16[144,512]{1,0:T(8,128)(2,1)S(1)}, bf16[144,512]{1,0:T(8,128)(2,1)S(1)}, u32[]{:S(2)}, u32[]{:S(2)}) collective-permute-start(bf16[144,512]{1,0:T(8,128)(2,1)S(1)} %get-tuple-element.55.refs_4_), channel_id=1, source_target_pairs={{0,16},{1,17},{2,18},{3,19},{4,20},{5,21},{6,22},{7,23},{8,24},{9,... | collective-permute-start | bytes 442376 | tf_op jit(solution)/shard_map/ppermute | solution.py:39
  32.2 12.8 %collective-permute-start.8 = (bf16[4,144,512]{2,1,0:T(8,128)(2,1)S(1)}, bf16[4,144,512]{2,1,0:T(8,128)(2,1)S(1)}, u32[]{:S(2)}, u32[]{:S(2)}) collective-permute-start(bf16[4,144,512]{2,1,0:T(8,128)(2,1)S(1)} %get-tuple-element.57.refs_0_), channel_id=1, source_target_pairs={{0,24},{1,25},{2,26},{3,27},{4,28},{5,29},{6,30},{7,31},{8,0},{9,1... | collective-permute-start | bytes 1769480 | tf_op jit(solution)/shard_map/ppermute | solution.py:39
  33.9 12.9 %collective-permute-start.11 = (bf16[4,144,512]{2,1,0:T(8,128)(2,1)S(1)}, bf16[4,144,512]{2,1,0:T(8,128)(2,1)S(1)}, u32[]{:S(2)}, u32[]{:S(2)}) collective-permute-start(bf16[4,144,512]{2,1,0:T(8,128)(2,1)S(1)} %get-tuple-element.59.refs_4_), channel_id=1, source_target_pairs={{0,3},{1,0},{2,1},{3,2},{4,7},{5,4},{6,5},{7,6},{8,11},{9,8},{10,9... | collective-permute-start | bytes 1769480 | tf_op jit(solution)/shard_map/ppermute | solution.py:35
  35.3 26.2 %collective-permute-start.10 = (bf16[4,144,512]{2,1,0:T(8,128)(2,1)S(1)}, bf16[4,144,512]{2,1,0:T(8,128)(2,1)S(1)}, u32[]{:S(2)}, u32[]{:S(2)}) collective-permute-start(bf16[4,144,512]{2,1,0:T(8,128)(2,1)S(1)} %get-tuple-element.57.refs_0_), channel_id=1, source_target_pairs={{0,8},{1,9},{2,10},{3,11},{4,12},{5,13},{6,14},{7,15},{8,16},{9,17... | collective-permute-start | bytes 1769480 | tf_op jit(solution)/shard_map/ppermute | solution.py:39
  35.7 26.0 %collective-permute-start.13 = (bf16[4,144,512]{2,1,0:T(8,128)(2,1)S(1)}, bf16[4,144,512]{2,1,0:T(8,128)(2,1)S(1)}, u32[]{:S(2)}, u32[]{:S(2)}) collective-permute-start(bf16[4,144,512]{2,1,0:T(8,128)(2,1)S(1)} %get-tuple-element.59.refs_4_), channel_id=1, source_target_pairs={{0,1},{1,2},{2,3},{3,0},{4,5},{5,6},{6,7},{7,4},{8,9},{9,10},{10,1... | collective-permute-start | bytes 1769480 | tf_op jit(solution)/shard_map/ppermute | solution.py:35
  45.0 16.8 %collective-permute-start.9 = (bf16[4,144,512]{2,1,0:T(8,128)(2,1)S(1)}, bf16[4,144,512]{2,1,0:T(8,128)(2,1)S(1)}, u32[]{:S(2)}, u32[]{:S(2)}) collective-permute-start(bf16[4,144,512]{2,1,0:T(8,128)(2,1)S(1)} %get-tuple-element.57.refs_0_), channel_id=1, source_target_pairs={{0,16},{1,17},{2,18},{3,19},{4,20},{5,21},{6,22},{7,23},{8,24},{9,... | collective-permute-start | bytes 1769480 | tf_op jit(solution)/shard_map/ppermute | solution.py:39
  46.8 14.9 %collective-permute-start.12 = (bf16[4,144,512]{2,1,0:T(8,128)(2,1)S(1)}, bf16[4,144,512]{2,1,0:T(8,128)(2,1)S(1)}, u32[]{:S(2)}, u32[]{:S(2)}) collective-permute-start(bf16[4,144,512]{2,1,0:T(8,128)(2,1)S(1)} %get-tuple-element.59.refs_4_), channel_id=1, source_target_pairs={{0,2},{1,3},{2,0},{3,1},{4,6},{5,7},{6,4},{7,5},{8,10},{9,11},{10,... | collective-permute-start | bytes 1769480 | tf_op jit(solution)/shard_map/ppermute | solution.py:35
  47.7 6.4 %collective-permute-start.14 = (bf16[144,512]{1,0:T(8,128)(2,1)S(1)}, bf16[144,512]{1,0:T(8,128)(2,1)S(1)}, u32[]{:S(2)}, u32[]{:S(2)}) collective-permute-start(bf16[144,512]{1,0:T(8,128)(2,1)S(1)} %convert_element_type.28), channel_id=1, source_target_pairs={{0,64},{32,96},{64,0},{96,32},{128,192},{160,224},{192,128},{224,1... | collective-permute-start | bytes 442376 | tf_op jit(solution)/shard_map/ppermute | solution.py:51
  54.1 14.0 %collective-permute-start.15 = (bf16[144,512]{1,0:T(8,128)(2,1)S(1)}, bf16[144,512]{1,0:T(8,128)(2,1)S(1)}, u32[]{:S(2)}, u32[]{:S(2)}) collective-permute-start(bf16[144,512]{1,0:T(8,128)(2,1)S(1)} %fusion.2), channel_id=1, source_target_pairs={{0,128},{32,160},{64,192},{96,224},{128,0},{160,32},{192,64},{224,... | collective-permute-start | bytes 442376 | tf_op jit(solution)/shard_map/ppermute | solution.py:51
  68.1 49.7 %collective-permute-start.16 = (bf16[13,256,256]{2,1,0:T(8,128)(2,1)}, bf16[13,256,256]{2,1,0:T(8,128)(2,1)}, u32[]{:S(2)}, u32[]{:S(2)}) collective-permute-start(bf16[13,256,256]{2,1,0:T(8,128)(2,1)} %partner_side.1), channel_id=1, source_target_pairs={{0,4},{1,5},{2,6},{3,7},{4,0},{5,1},{6,2},{7,3},{8,12},{9,13},{10,... | collective-permute-start | bytes 5111816 | tf_op jit(solution)/shard_map/ppermute | solution.py:43
  68.6 16.4 %collective-permute-start.17 = (bf16[4,144,512]{2,1,0:T(8,128)(2,1)S(1)}, bf16[4,144,512]{2,1,0:T(8,128)(2,1)S(1)}, u32[]{:S(2)}, u32[]{:S(2)}) collective-permute-start(bf16[4,144,512]{2,1,0:T(8,128)(2,1)S(1)} %get-tuple-element.68), channel_id=1, source_target_pairs={{0,8},{1,9},{2,10},{3,11},{4,12},{5,13},{6,14},{7,15},{8,16},{9,17... | collective-permute-start | bytes 1769480 | tf_op jit(solution)/shard_map/ppermute | solution.py:39
  69.7 16.5 %collective-permute-start.20 = (bf16[4,144,512]{2,1,0:T(8,128)(2,1)S(1)}, bf16[4,144,512]{2,1,0:T(8,128)(2,1)S(1)}, u32[]{:S(2)}, u32[]{:S(2)}) collective-permute-start(bf16[4,144,512]{2,1,0:T(8,128)(2,1)S(1)} %get-tuple-element.73), channel_id=1, source_target_pairs={{0,1},{1,2},{2,3},{3,0},{4,5},{5,6},{6,7},{7,4},{8,9},{9,10},{10,1... | collective-permute-start | bytes 1769480 | tf_op jit(solution)/shard_map/ppermute | solution.py:35
  71.7 24.1 %collective-permute-start.19 = (bf16[4,144,512]{2,1,0:T(8,128)(2,1)S(1)}, bf16[4,144,512]{2,1,0:T(8,128)(2,1)S(1)}, u32[]{:S(2)}, u32[]{:S(2)}) collective-permute-start(bf16[4,144,512]{2,1,0:T(8,128)(2,1)S(1)} %get-tuple-element.71), channel_id=1, source_target_pairs={{0,24},{1,25},{2,26},{3,27},{4,28},{5,29},{6,30},{7,31},{8,0},{9,1... | collective-permute-start | bytes 1769480 | tf_op jit(solution)/shard_map/ppermute | solution.py:39
  75.0 20.9 %collective-permute-start.22 = (bf16[4,144,512]{2,1,0:T(8,128)(2,1)S(1)}, bf16[4,144,512]{2,1,0:T(8,128)(2,1)S(1)}, u32[]{:S(2)}, u32[]{:S(2)}) collective-permute-start(bf16[4,144,512]{2,1,0:T(8,128)(2,1)S(1)} %get-tuple-element.76), channel_id=1, source_target_pairs={{0,3},{1,0},{2,1},{3,2},{4,7},{5,4},{6,5},{7,6},{8,11},{9,8},{10,9... | collective-permute-start | bytes 1769480 | tf_op jit(solution)/shard_map/ppermute | solution.py:35
  85.0 15.0 %collective-permute-start.18 = (bf16[4,144,512]{2,1,0:T(8,128)(2,1)S(1)}, bf16[4,144,512]{2,1,0:T(8,128)(2,1)S(1)}, u32[]{:S(2)}, u32[]{:S(2)}) collective-permute-start(bf16[4,144,512]{2,1,0:T(8,128)(2,1)S(1)} %get-tuple-element.70), channel_id=1, source_target_pairs={{0,16},{1,17},{2,18},{3,19},{4,20},{5,21},{6,22},{7,23},{8,24},{9,... | collective-permute-start | bytes 1769480 | tf_op jit(solution)/shard_map/ppermute | solution.py:39
  86.2 15.0 %collective-permute-start.21 = (bf16[4,144,512]{2,1,0:T(8,128)(2,1)S(1)}, bf16[4,144,512]{2,1,0:T(8,128)(2,1)S(1)}, u32[]{:S(2)}, u32[]{:S(2)}) collective-permute-start(bf16[4,144,512]{2,1,0:T(8,128)(2,1)S(1)} %get-tuple-element.75), channel_id=1, source_target_pairs={{0,2},{1,3},{2,0},{3,1},{4,6},{5,7},{6,4},{7,5},{8,10},{9,11},{10,... | collective-permute-start | bytes 1769480 | tf_op jit(solution)/shard_map/ppermute | solution.py:35
  95.9 17.5 %collective-permute-start.29 = (f32[144,512]{1,0:T(8,128)}, f32[144,512]{1,0:T(8,128)}, u32[]{:S(2)}, u32[]{:S(2)}) collective-permute-start(f32[144,512]{1,0:T(8,128)} %broadcast_multiply_fusion), channel_id=1, source_target_pairs={{0,32},{32,0},{64,96},{96,64},{128,160},{160,128},{192,224},{224,1... | collective-permute-start | bytes 884744 | tf_op jit(solution)/shard_map/ppermute | solution.py:47
  102.8 6.6 %collective-permute-start.23 = (bf16[144,512]{1,0:T(8,128)(2,1)}, bf16[144,512]{1,0:T(8,128)(2,1)S(1)}, u32[]{:S(2)}, u32[]{:S(2)}) collective-permute-start(bf16[144,512]{1,0:T(8,128)(2,1)} %get-tuple-element.78), channel_id=1, source_target_pairs={{0,1},{1,2},{2,3},{3,0},{4,5},{5,6},{6,7},{7,4},{8,9},{9,10},{10,1... | collective-permute-start | bytes 442376 | tf_op jit(solution)/shard_map/ppermute | solution.py:35
  103.7 7.2 %collective-permute-start.26 = (bf16[144,512]{1,0:T(8,128)(2,1)}, bf16[144,512]{1,0:T(8,128)(2,1)S(1)}, u32[]{:S(2)}, u32[]{:S(2)}) collective-permute-start(bf16[144,512]{1,0:T(8,128)(2,1)} %get-tuple-element.83), channel_id=1, source_target_pairs={{0,8},{1,9},{2,10},{3,11},{4,12},{5,13},{6,14},{7,15},{8,16},{9,17... | collective-permute-start | bytes 442376 | tf_op jit(solution)/shard_map/ppermute | solution.py:39
  104.5 20.2 %collective-permute-start.25 = (bf16[144,512]{1,0:T(8,128)(2,1)}, bf16[144,512]{1,0:T(8,128)(2,1)S(1)}, u32[]{:S(2)}, u32[]{:S(2)}) collective-permute-start(bf16[144,512]{1,0:T(8,128)(2,1)} %copy-done.11), channel_id=1, source_target_pairs={{0,3},{1,0},{2,1},{3,2},{4,7},{5,4},{6,5},{7,6},{8,11},{9,8},{10,9... | collective-permute-start | bytes 442376 | tf_op jit(solution)/shard_map/ppermute | solution.py:35
  109.5 15.2 %collective-permute-start.28 = (bf16[144,512]{1,0:T(8,128)(2,1)}, bf16[144,512]{1,0:T(8,128)(2,1)S(1)}, u32[]{:S(2)}, u32[]{:S(2)}) collective-permute-start(bf16[144,512]{1,0:T(8,128)(2,1)} %copy-done.10), channel_id=1, source_target_pairs={{0,24},{1,25},{2,26},{3,27},{4,28},{5,29},{6,30},{7,31},{8,0},{9,1... | collective-permute-start | bytes 442376 | tf_op jit(solution)/shard_map/ppermute | solution.py:39
  110.9 13.8 %collective-permute-start.24 = (bf16[144,512]{1,0:T(8,128)(2,1)}, bf16[144,512]{1,0:T(8,128)(2,1)S(1)}, u32[]{:S(2)}, u32[]{:S(2)}) collective-permute-start(bf16[144,512]{1,0:T(8,128)(2,1)} %copy-done.9), channel_id=1, source_target_pairs={{0,2},{1,3},{2,0},{3,1},{4,6},{5,7},{6,4},{7,5},{8,10},{9,11},{10,... | collective-permute-start | bytes 442376 | tf_op jit(solution)/shard_map/ppermute | solution.py:35
  113.4 11.3 %collective-permute-start.27 = (bf16[144,512]{1,0:T(8,128)(2,1)}, bf16[144,512]{1,0:T(8,128)(2,1)S(1)}, u32[]{:S(2)}, u32[]{:S(2)}) collective-permute-start(bf16[144,512]{1,0:T(8,128)(2,1)} %copy-done.8), channel_id=1, source_target_pairs={{0,16},{1,17},{2,18},{3,19},{4,20},{5,21},{6,22},{7,23},{8,24},{9,... | collective-permute-start | bytes 442376 | tf_op jit(solution)/shard_map/ppermute | solution.py:39
  (13 other events, 90.5 us)
